TPU v7x, 512 devices: a whole 4x4x16 slice. The times are simulated.
512 devices in a mesh: section: 64 (over z, y_lo, core), tensor: 8 (over x, y_hi).
Axes of the slice: x: 4, y: 4 (y_hi: 2, y_lo: 2; y = y_hi * 2 + y_lo), z: 16, core: 2. Of those that a mesh axis runs over, the one named last changes fastest.
Arguments:
- state_coef: bfloat16 [64, 384, 512], P('section'), may hold values from -12 to 12
- embed_terms: bfloat16 [64, 2, 384, 8192], P('section', None, None, 'tensor'), may hold values from -4 to 4
- norm_gain: bfloat16 [64, 8192], P('section', 'tensor'), may hold values from 0.099609375 to 1.8984375
- w_query: bfloat16 [64, 8192, 512], P('section', 'tensor'), may hold values from -0.055242717 to 0.055242717
- w_keyval: bfloat16 [64, 8192, 256], P('section', 'tensor'), may hold values from -0.055242717 to 0.055242717
- w_out: bfloat16 [64, 512, 8192], P('section', None, 'tensor'), may hold values from -0.25 to 0.25
- basis: bfloat16 [8192, 512], P('tensor'), may hold values from -0.0625 to 0.0625
- doc_lengths: int32 [64, 2, 4], P('section'), may hold values from 1 to 192, 384 in all within a row
Outputs:
- boundary: bfloat16 [64, 2, 384, 512], P('section')
Inputs may be any that keep to these rules, and one draw needn't show every extreme that they name: `doc_lengths`: each row holds 4 lengths summing to 384; its largest is 192.
All inputs are finite; a program needn't handle non-finite values.
Results may differ from a plain program's by a relative error of at most 0.007.
Values may be sent and summed in bfloat16 or wider, within the bound.
No kernel may reach another device: no remote copies, remote signals or barrier semaphores. Data moves between devices by JAX's collectives and lax.ppermute only.
A program may use at most 64 MiB of HBM per device.

v0:
```python
import jax
import jax.numpy as jnp
from jax import lax
from jax.sharding import PartitionSpec as P

HEAD = 128
GROUP = 4
TICKS = 2


def from_behind(shard, axis, by):
    count = lax.axis_size(axis)
    pairs = [(i, i + by) for i in range(count) if 0 <= i + by < count]
    return lax.ppermute(shard, axis, pairs)


def doc_layout(lengths, length_total):
    indices = jnp.arange(length_total, dtype=jnp.int32)
    doc_ends = jnp.cumsum(lengths)
    segment = jnp.sum((indices[:, None] >= doc_ends[None, :]).astype(jnp.int32), axis=1)
    starts = doc_ends - lengths
    chosen = segment[:, None] == jnp.arange(lengths.shape[0], dtype=jnp.int32)[None, :]
    begin = jnp.sum(jnp.where(chosen, starts[None, :], 0), axis=1)
    return (segment, (indices - begin).astype(jnp.float32))


def rotate_heads(block, position):
    half_head = HEAD // 2
    frequency = 500000.0 ** (-(jnp.arange(half_head, dtype=jnp.float32) * 2.0) / HEAD)
    angles = position[:, None, None] * frequency[None, None, :]
    cosine = jnp.cos(angles)
    sine_part = jnp.sin(angles)
    first_half = block[..., :half_head]
    second_half = block[..., half_head:]
    return jnp.concatenate(
        [
            first_half * cosine - second_half * sine_part,
            second_half * cosine + first_half * sine_part,
        ],
        axis=-1,
    )


def embed_positions(block, position):
    count_rows = block.shape[0]
    width_q = GROUP * HEAD
    queries = rotate_heads(block[:, :width_q].reshape(count_rows, GROUP, HEAD), position)
    key_head = rotate_heads(
        block[:, width_q : width_q + HEAD].reshape(count_rows, 1, HEAD), position
    )
    return jnp.concatenate(
        [
            queries.reshape(count_rows, width_q),
            key_head.reshape(count_rows, HEAD),
            block[:, width_q + HEAD :],
        ],
        axis=1,
    ).astype(jnp.bfloat16)


def attend(combined, segment):
    count_rows = combined.shape[0]
    width_q = GROUP * HEAD
    queries = combined[:, :width_q].reshape(count_rows, GROUP, HEAD)
    keys = combined[:, width_q : width_q + HEAD]
    values = combined[:, width_q + HEAD :]
    scores = jnp.einsum(
        "sgh,th->gst", queries, keys, preferred_element_type=jnp.float32
    ) * HEAD ** (-0.5)
    indices = jnp.arange(count_rows, dtype=jnp.int32)
    allowed = (segment[:, None] == segment[None, :]) & (indices[None, :] <= indices[:, None])
    scores = jnp.where(allowed[None], scores, -1e30)
    peak = jnp.max(scores, axis=-1, keepdims=True)
    expo = jnp.exp(scores - peak)
    weights = (expo / jnp.sum(expo, axis=-1, keepdims=True)).astype(jnp.bfloat16)
    result = jnp.einsum("gst,th->sgh", weights, values, preferred_element_type=jnp.float32)
    return result.reshape(count_rows, width_q).astype(jnp.bfloat16)


def local(state_coef, embed_terms, norm_gain, w_query, w_keyval, w_out, basis, doc_lengths):
    coef_now = state_coef[0]
    row_count = coef_now.shape[0]
    gain_row = norm_gain[0].astype(jnp.float32)
    full_width = embed_terms.shape[-1] * lax.axis_size("tensor")
    w_q = w_query[0]
    w_kv = w_keyval[0]
    w_o = w_out[0]
    produced = []
    for step_index in range(TICKS):
        embedded = embed_terms[0, step_index]
        lifted = jnp.dot(coef_now, basis.T, preferred_element_type=jnp.float32)
        stream = embedded.astype(jnp.float32) + lifted
        squares = lax.psum(jnp.sum(stream * stream, axis=-1), "tensor")
        inverse = lax.rsqrt(squares / full_width + 1e-05)
        normed = (stream * inverse[:, None] * gain_row).astype(jnp.bfloat16)
        segment, position = doc_layout(doc_lengths[0, step_index], row_count)
        queries = jnp.dot(normed, w_q, preferred_element_type=jnp.float32)
        keyval = jnp.dot(normed, w_kv, preferred_element_type=jnp.float32)
        queries, keyval = lax.psum((queries, keyval), "tensor")
        combined = embed_positions(jnp.concatenate([queries, keyval], axis=1), position)
        attended = attend(combined, segment)
        attn_out = jnp.dot(attended, w_o, preferred_element_type=jnp.float32)
        carried = (lifted + attn_out).astype(jnp.bfloat16)
        partial_coef = jnp.dot(carried, basis, preferred_element_type=jnp.float32)
        gathered_coef = lax.psum(partial_coef, "tensor").astype(jnp.bfloat16)
        produced.append(gathered_coef)
        if step_index + 1 < TICKS:
            coef_now = from_behind(gathered_coef, "section", 1)
    return jnp.stack(produced, axis=0)[None]


def solution(mesh):
    return jax.shard_map(
        local,
        mesh=mesh,
        in_specs=(
            P("section", None, None),
            P("section", None, None, "tensor"),
            P("section", "tensor"),
            P("section", "tensor", None),
            P("section", "tensor", None),
            P("section", None, "tensor"),
            P("tensor", None),
            P("section", None, None),
        ),
        out_specs=P("section", None, None, None),
        check_vma=False,
    )
```

profile of v0, /device:TPU:2, one launch (start us, length us, event | category | flops | bytes accessed | tf_op | source)
XLA Modules:
  0.0 421.9 jit_solution(5540555607071939713)
XLA Ops:
  6.5 0.0 copy-start
  6.5 0.0 all-reduce.9.cloned.1.call-start
  6.5 0.8 mul.275
  7.3 0.5 copy-done
  7.8 1.9 multiply_reduce_fusion.1
  9.7 22.2 %psum.56 = f32[384]{0:T(512)S(1)} all-reduce(f32[384]{0:T(512)S(1)} %get-tuple-element.27), channel_id=1, replica_groups=mesh['section'=64,'tensor'=8] {'tensor'}, use_global_device_ids=true, to_apply=%region_1.0 | all-reduce | flops 384 | bytes 3072 | tf_op jit(solution)/shard_map/psum | solution.py:93
  31.9 1.4 multiply_convert_fusion.1
  33.4 0.0 copy-done.3
  33.4 0.0 copy-start.1
  33.4 1.2 fusion.22
  34.7 0.0 copy-done.1
  34.7 0.6 convolution_bitcast_fusion.1
  35.2 0.0 copy-start.10
  35.2 0.9 copy.42
  36.2 0.0 all-reduce.9.cloned.1.call-update
  36.2 0.0 all-reduce.7.cloned.1.call-start
  36.3 0.0 copy-done.10
  36.3 0.2 reduce-window.15
  36.5 0.2 reduce-window.14
  36.6 0.1 convert_reduce_fusion
  36.7 0.1 convert_reduce_fusion.1
  36.8 0.1 select_reduce_fusion
  36.9 0.1 select_reduce_fusion.1
  37.0 0.8 fusion.19
  37.8 0.0 copy-done.8
  37.8 2.1 multiply_cosine_fusion
  39.9 102.4 %all-reduce.9.cloned.1.call-done = (f32[384,4,128]{2,0,1:T(8,128)}, f32[384,256]{0,1:T(8,128)}) async-done(((f32[384,4,128]{2,0,1:T(8,128)}, f32[384,256]{0,1:T(8,128)}), (f32[384,4,128]{2,0,1:T(8,128)}, f32[384,256]{0,1:T(8,128)})) %all-reduce.9.cloned.1.call-update) | async-done | bytes 1179664 | tf_op jit(solution)/shard_map/psum | solution.py:99
  142.3 0.9 slice_bitcast_fusion.1
  143.3 1.7 fusion.55
  145.0 2.6 subtract_convert_fusion.1
  147.6 4.3 %fusion.76 = (f32[4,384]{1,0:T(4,128)}, f32[4,384,384]{1,2,0:T(8,128)}) fusion(pred[384,384]{0,1:T(8,128)(4,1)} %fusion.19, bf16[384,4,64]{2,0,1:T(8,128)(2,1)} %get-tuple-element.12, bf16[384,4,64]{2,0,1:T(8,128)(2,1)} %get-tuple-element.11, bf16[384,1,64]{0,2,1:T(8,128)(2,1)} %get-tuple-element.16, bf16[384,1,64]{0,2,1:T(8,128)(2,1)} %get-tuple-element.15), kind=kOutput, calls=%fused_computation.116 | convolution fusion | flops 154337664 | bytes 3004416 | tf_op jit(solution)/shard_map/sub | solution.py:74
  151.9 0.0 copy-done.6
  151.9 2.8 convolution_convert_fusion.1
  154.7 3.2 fusion.4
  157.9 49.9 %all-reduce.10 = bf16[384,512]{1,0:T(8,128)(2,1)S(1)} all-reduce(f32[384,512]{1,0:T(8,128)} %fusion.4), channel_id=1, replica_groups=mesh['section'=64,'tensor'=8] {'tensor'}, use_global_device_ids=true, to_apply=%region_9.10 | all-reduce | flops 196608 | bytes 1179648 | tf_op jit(solution)/shard_map/psum | solution.py:105
  207.8 1.3 collective-permute-start
  209.1 1.3 collective-permute-done
  210.4 1.8 multiply_reduce_fusion
  212.2 22.2 %psum.60 = f32[384]{0:T(512)} all-reduce(f32[384]{0:T(512)S(1)} %get-tuple-element.31), channel_id=1, replica_groups=mesh['section'=64,'tensor'=8] {'tensor'}, use_global_device_ids=true, to_apply=%region_11.12 | all-reduce | flops 384 | bytes 3072 | tf_op jit(solution)/shard_map/psum | solution.py:93
  234.5 0.7 add_rsqrt_fusion
  235.2 1.4 multiply_convert_fusion
  236.6 0.0 copy-start.2
  236.6 1.2 fusion.20
  237.8 0.0 copy-done.2
  237.8 0.6 convolution_bitcast_fusion
  238.4 0.0 copy-start.9
  238.4 0.0 copy-start.4
  238.4 0.0 copy-start.5
  238.4 0.9 copy.41
  239.4 0.0 all-reduce.7.cloned.1.call-update
  239.4 0.8 fusion.18
  240.2 110.4 %all-reduce.7.cloned.1.call-done = (f32[384,4,128]{2,0,1:T(8,128)}, f32[384,256]{0,1:T(8,128)}) async-done(((f32[384,4,128]{2,0,1:T(8,128)}, f32[384,256]{0,1:T(8,128)}), (f32[384,4,128]{2,0,1:T(8,128)}, f32[384,256]{0,1:T(8,128)})) %all-reduce.7.cloned.1.call-update) | async-done | bytes 1179664 | tf_op jit(solution)/shard_map/psum | solution.py:99
  350.6 0.9 slice_bitcast_fusion
  351.5 0.0 copy-done.9
  351.5 0.4 fusion.51
  352.0 0.0 copy-done.4
  352.0 0.0 copy-done.5
  352.0 2.6 subtract_convert_fusion
  354.6 3.7 fusion.79
  358.3 0.0 copy-done.7
  358.3 2.8 convolution_convert_fusion
  361.1 3.2 fusion.5
  364.3 49.9 %all-reduce.11 = bf16[384,512]{1,0:T(8,128)(2,1)S(1)} all-reduce(f32[384,512]{1,0:T(8,128)} %fusion.5), channel_id=1, replica_groups=mesh['section'=64,'tensor'=8] {'tensor'}, use_global_device_ids=true, to_apply=%region_19.20 | all-reduce | flops 196608 | bytes 1179648 | tf_op jit(solution)/shard_map/psum | solution.py:105
  414.2 0.9 maximum_bitcast_fusion
  (10 shorter events, 0.0 us)
Async XLA Ops:
  6.5 1.2 copy-start
  6.5 135.8 %all-reduce.9.cloned.1.call-start = ((), (), s32[]{:S(2)}) async-start(), calls=%async_computation.1 | async-start | bytes 2359296 | tf_op jit(solution)/shard_map/psum | solution.py:99
  31.9 1.5 copy-start.3
  33.4 1.3 copy-start.1
  35.2 1.0 copy-start.10
  36.2 314.4 %all-reduce.7.cloned.1.call-start = ((), (), s32[]{:S(2)}) async-start(), calls=%async_computation | async-start | bytes 2359296 | tf_op jit(solution)/shard_map/psum | solution.py:99
  36.8 1.0 copy-start.8
  147.6 4.3 %copy-start.6 = (f32[384,256]{0,1:T(8,128)S(1)}, f32[384,256]{0,1:T(8,128)}, u32[]{:S(2)}) copy-start(f32[384,256]{0,1:T(8,128)} %get-tuple-element.8) | copy-start | bytes 1179652
  207.8 2.6 collective-permute-start
  236.6 1.3 copy-start.2
  238.4 113.1 %copy-start.9 = (f32[64]{0:T(128)S(1)}, f32[64]{0:T(128)}, u32[]{:S(2)}) copy-start(f32[64]{0:T(128)} %copy-done.8) | copy-start | bytes 772
  238.4 113.6 %copy-start.4 = (f32[384,64]{1,0:T(8,128)S(1)}, f32[384,64]{1,0:T(8,128)}, u32[]{:S(2)}) copy-start(f32[384,64]{1,0:T(8,128)} %get-tuple-element.17) | copy-start | bytes 294916
  238.4 113.6 %copy-start.5 = (f32[384,64]{1,0:T(8,128)S(1)}, f32[384,64]{1,0:T(8,128)}, u32[]{:S(2)}) copy-start(f32[384,64]{1,0:T(8,128)} %get-tuple-element.18) | copy-start | bytes 294916
  354.6 3.7 copy-start.7
Sparse Core Ops, SparseCore 0:
  36.3 105.9 all-reduce.8
  239.5 111.0 all-reduce.6
where the time goes:
time: 423 us; the launch traced here: 422 us
  waiting for transfers between devices  214 us (51%)
  blocking collectives  144 us (34%)
  matrix products  27.4 us (6%)
  other arithmetic  17 us (4%)
  between operations  13.6 us (3%)
  local copies, waits for them, and re-layouts  4.25 us (1%)
    psum x2, waiting for transfers between devices, local(): queries, keyval = lax.psum((queries, keyval), 'tensor')  213 us
    psum x2, blocking collectives, local(): gathered_coef = lax.psum(partial_coef, 'tensor').astype(jnp.bfloat16)  99.7 us
    psum x2, blocking collectives, local(): squares = lax.psum(jnp.sum(stream * stream, axis=-1), 'tensor')  44.4 us
  transfers between devices with their start and end apart: 3, of which 3 were waited for; matrix products, arithmetic and copies ran while one was open for 1% of the time, Pallas kernels for 0%

commit v1 on v0

v1 whole, which is shorter than its diff:
```python
import functools
import math

import jax
import jax.numpy as jnp
from jax import lax
from jax.experimental import pallas as pl
from jax.experimental.pallas import tpu as pltpu
from jax.sharding import PartitionSpec as P

HEAD = 128
GROUP = 4
WIDTH_Q = GROUP * HEAD
WIDTH = WIDTH_Q + 2 * HEAD
PARTS = 8
ROWS = 384
OWN = ROWS // PARTS
RANK = 512
PANEL = 256
M_OWN = RANK // PARTS
G_OWN = HEAD // PARTS
BF16 = jnp.bfloat16
F32 = jnp.float32
MIB = 1024 * 1024
LIMIT0 = 56

QKV_ROWS = OWN * (WIDTH // HEAD)
M_AT = QKV_ROWS
G_AT = M_AT + M_OWN * (RANK // HEAD)
G_BLOCKS = ((0, 0), (0, 1), (1, 1), (2, 2), (2, 3), (3, 3), (0, 2), (0, 3), (1, 2), (1, 3))
MIXED_ROWS = G_AT + len(G_BLOCKS) * G_OWN
TAIL = 16

VMEM = pl.BlockSpec(memory_space=pltpu.VMEM)
SMEM = pl.BlockSpec(memory_space=pltpu.SMEM)
ANY = pl.BlockSpec(memory_space=pl.ANY)
HBM = pl.BlockSpec(memory_space=pltpu.HBM)


def call(body, name, out_shape, in_specs, flops, moved, args, scratch=(), out_specs=VMEM, limit=16):
    return pl.pallas_call(
        body,
        name=name,
        out_shape=out_shape,
        in_specs=in_specs,
        out_specs=out_specs,
        scratch_shapes=scratch,
        cost_estimate=pl.CostEstimate(flops=flops, bytes_accessed=moved, transcendentals=0),
        compiler_params=pltpu.CompilerParams(vmem_limit_bytes=limit * MIB),
    )(*args)


def dot(a, b):
    return jnp.dot(a, b, preferred_element_type=F32)


def dot_t(a, b):
    return lax.dot_general(a, b, (((1,), (1,)), ((), ())), preferred_element_type=F32)


def column_to_row(column):
    shape = (column.shape[0], HEAD)
    row = lax.broadcasted_iota(jnp.int32, shape, 0)
    lane = lax.broadcasted_iota(jnp.int32, shape, 1)
    return jnp.sum(jnp.where(row == lane, column, 0.0), axis=0, keepdims=True)


def row_to_column(row_vector, rows):
    row = lax.broadcasted_iota(jnp.int32, (rows, HEAD), 0)
    lane = lax.broadcasted_iota(jnp.int32, (rows, HEAD), 1)
    return jnp.sum(jnp.where(row == lane, row_vector, 0.0), axis=1, keepdims=True)


def pack(out, value, at, rows):
    for column in range(value.shape[1] // HEAD):
        part = value[:, column * HEAD : (column + 1) * HEAD]
        for to in range(PARTS):
            out[to, at + column * rows : at + (column + 1) * rows, :] = part[
                to * rows : (to + 1) * rows
            ]


def unpack(packed, at, rows, columns=1):
    parts = [
        packed[:, at + column * rows : at + (column + 1) * rows, :].reshape(PARTS * rows, HEAD)
        for column in range(columns)
    ]
    return parts[0] if columns == 1 else jnp.concatenate(parts, axis=1)


def qkv_sums(stream, squares, gain, weights, ready, buffer):
    tail_at = buffer.shape[1] - TAIL
    scaled = (stream * gain.astype(F32)).astype(BF16)
    row = lax.broadcasted_iota(jnp.int32, (TAIL, HEAD), 0)
    for to in range(PARTS):
        laid = column_to_row(squares[to * OWN : (to + 1) * OWN])
        high = laid.astype(BF16).astype(F32)
        value = jnp.where(row == 0, high, jnp.where(row == 1, laid - high, 0.0))
        buffer[to, tail_at:, :] = value.astype(BF16)
    ready()
    w_q, w_kv = weights
    for panel in range(WIDTH // PANEL):
        if panel < WIDTH_Q // PANEL:
            weight = w_q[:, panel * PANEL : (panel + 1) * PANEL]
        else:
            weight = w_kv[...]
        pack(buffer, dot(scaled, weight).astype(BF16), panel * OWN * (PANEL // HEAD), OWN)


def rotary_tables(lengths, tables):
    lane = lax.broadcasted_iota(jnp.int32, (OWN, HEAD), 1)
    half = HEAD // 2
    pair = jnp.where(lane < half, lane, lane - half).astype(F32)
    frequency = jnp.exp(pair * (-math.log(500000.0) / half))
    index = lax.broadcasted_iota(jnp.int32, (OWN, HEAD), 0) + lax.axis_index("tensor") * OWN
    for step in range(2):
        end, begin = 0, jnp.zeros((OWN, HEAD), jnp.int32)
        for document in range(3):
            end = end + lengths[0, step, document]
            begin = jnp.where(index >= end, end, begin)
        angle = (index - begin).astype(F32) * frequency
        sine = jnp.sin(angle)
        tables[2 * step] = jnp.cos(angle)
        tables[2 * step + 1] = jnp.where(lane < half, -sine, sine)


def symmetric_sums(basis, buffer):
    left, right = basis[:, :PANEL], basis[:, PANEL:]
    turned = left.T
    parts = {
        (0, 0): dot(turned, left).astype(BF16),
        (0, 2): dot(turned, right).astype(BF16),
        (2, 2): dot(right.T, right).astype(BF16),
    }
    for place, (row, column) in enumerate(G_BLOCKS):
        part = parts[(row // 2 * 2, column // 2 * 2)]
        row, column = row % 2 * HEAD, column % 2 * HEAD
        block = part[row : row + HEAD, column : column + HEAD]
        pack(buffer, block, G_AT + place * G_OWN, G_OWN)


def symmetric_blocks(packed):
    blocks = {
        pair: unpack(packed, G_AT + place * G_OWN, G_OWN) for place, pair in enumerate(G_BLOCKS)
    }

    def part(row, column):
        corner = (
            blocks[(row + 1, column)] if row != column else blocks[(row, column + 1)].T
        )
        upper = jnp.concatenate([blocks[(row, column)], blocks[(row, column + 1)]], axis=1)
        lower = jnp.concatenate([corner, blocks[(row + 1, column + 1)]], axis=1)
        return jnp.concatenate([upper, lower], axis=0)

    return part(0, 0), part(0, 2), part(2, 2)


def project0_kernel(
    lengths_in, basis_in, wo_in, coef_in, emb_in, gain_in, wq_in, wkv_in, out, tables,
    lengths, basis, w_o, coef, emb, gain, w_q, w_kv, sems,
):
    pairs = [
        (lengths_in, lengths), (basis_in, basis), (wo_in, w_o), (coef_in, coef),
        (emb_in.at[0, 0], emb), (gain_in, gain), (wq_in, w_q), (wkv_in, w_kv),
    ]
    copies = [
        pltpu.make_async_copy(source, target, sems.at[i])
        for i, (source, target) in enumerate(pairs)
    ]
    for copy in copies[:3]:
        copy.start()
    copies[0].wait()
    for copy in copies[3:]:
        copy.start()
    rotary_tables(lengths, tables)
    copies[1].wait()
    copies[2].wait()
    pack(out, dot(w_o[...], basis[...]).astype(BF16), M_AT, M_OWN)
    symmetric_sums(basis, out)
    for copy in copies[3:6]:
        copy.wait()
    stream = emb[...].astype(F32) + dot_t(coef[...], basis[...])
    squares = jnp.sum(stream * stream, axis=-1, keepdims=True)

    def ready():
        for copy in copies[6:]:
            copy.wait()

    qkv_sums(stream, squares, gain[...], (w_q, w_kv), ready, out)


def project1_kernel(coef_a, coef_b, gain, basis, emb, w_q, w_kv, out):
    coef = coef_a[...] + coef_b[...]
    stream = emb[0, 1].astype(F32) + dot_t(coef, basis[...])
    squares = jnp.sum(stream * stream, axis=-1, keepdims=True)
    qkv_sums(stream, squares, gain[...], (w_q, w_kv), lambda: None, out)


def turn(value, cosine, sine):
    return value * cosine + pltpu.roll(value, HEAD // 2, 1) * sine


def finish_kernel(width, step, parts, tables, out):
    def total(at, rows):
        value = parts[0, at : at + rows, :].astype(F32)
        for source in range(1, PARTS):
            value += parts[source, at : at + rows, :].astype(F32)
        return value

    for at in range(QKV_ROWS, out.shape[1], 16):
        value = total(at, 16).astype(BF16)
        for to in range(PARTS):
            out[to, at : at + 16, :] = value
    cosine, sine = tables[2 * step], tables[2 * step + 1]
    tail = total(parts.shape[1] - TAIL, TAIL)
    squares = row_to_column(tail[0:1] + tail[1:2], OWN)
    inverse = lax.rsqrt(squares * (1.0 / width) + 1e-05)
    for head in range(WIDTH // HEAD):
        rows = slice(head * OWN, (head + 1) * OWN)
        value = total(head * OWN, OWN) * inverse
        if head <= GROUP:
            value = turn(value, cosine, sine)
        value = value.astype(BF16)
        for to in range(PARTS):
            out[to, rows, :] = value


def attention(gathered, lengths, attended):
    first = lengths[0]
    second = first + lengths[1]
    third = second + lengths[2]
    heads = [unpack(gathered, head * OWN, OWN) for head in range(WIDTH // HEAD)]
    for tile in range(ROWS // HEAD):
        at = tile * HEAD
        count = at + HEAD
        queries = jnp.concatenate([heads[h][at:count] for h in range(GROUP)], axis=0)
        keys = heads[GROUP][:count]
        values = jnp.concatenate([heads[GROUP + 1][:count], jnp.ones((count, HEAD), BF16)], axis=1)
        row = lax.broadcasted_iota(jnp.int32, (HEAD, count), 0) + at
        column = lax.broadcasted_iota(jnp.int32, (HEAD, count), 1)
        begin = jnp.where(row >= first, first, 0)
        begin = jnp.where(row >= second, second, begin)
        begin = jnp.where(row >= third, third, begin)
        allowed = (column >= begin) & (column <= row)
        scores = dot_t(queries, keys) * HEAD ** (-0.5)
        for h in range(GROUP):
            own = jnp.where(allowed, scores[h * HEAD : (h + 1) * HEAD], -1e30)
            weights = jnp.exp(own - jnp.max(own, axis=-1, keepdims=True)).astype(BF16)
            summed = dot(weights, values)
            attended[at:count, h * HEAD : (h + 1) * HEAD] = (
                summed[:, :HEAD] / summed[:, HEAD:]
            ).astype(BF16)


def boundary_panels(coef, attended, mixed):
    first, second = coef[:, :PANEL], coef[:, PANEL:]
    upper, cross, lower = symmetric_blocks(mixed)
    of_g = (dot(first, upper) + dot_t(second, cross), dot(first, cross) + dot(second, lower))
    columns = PANEL // HEAD
    return [
        (of_g[panel] + dot(attended[...], unpack(mixed, M_AT + panel * columns * M_OWN, M_OWN, columns))).astype(BF16)
        for panel in range(RANK // PANEL)
    ]


def first_kernel(parity, gathered, coef, lengths, out, attended):
    @pl.when(lax.axis_index("section") % 2 == parity)
    def _():
        attention(gathered, [lengths[0, 0, i] for i in range(3)], attended)
        for panel, value in enumerate(boundary_panels(coef, attended, gathered)):
            out[:, panel * PANEL : (panel + 1) * PANEL] = value


def second_kernel(
    gathered, mixed, coef_a, coef_b, before_odd, before_even, lengths, out, attended, buffer, sems
):
    odd = lax.axis_index("section") % 2 == 1

    @pl.when(odd)
    def _():
        buffer[0] = before_odd[...]

    @pl.when(jnp.logical_not(odd))
    def _():
        buffer[0] = before_even[...]

    copies = [pltpu.make_async_copy(buffer.at[0], out.at[0], sems.at[0])]
    copies[0].start()
    coef = coef_a[...] + coef_b[...]
    attention(gathered, [lengths[0, 1, i] for i in range(3)], attended)
    for panel, value in enumerate(boundary_panels(coef, attended, mixed)):
        columns = pl.ds(panel * PANEL, PANEL)
        buffer[1, :, columns] = value
        copies.append(
            pltpu.make_async_copy(
                buffer.at[1, :, columns], out.at[1, :, columns], sems.at[1 + panel]
            )
        )
        copies[-1].start()
    for copy in copies:
        copy.wait()


def exchange(blocks):
    return lax.all_to_all(blocks, "tensor", 0, 0)


def hop(value, parity):
    sections = lax.axis_size("section")
    pairs = [(s, s + 1) for s in range(sections - 1) if s % 2 == parity]
    return lax.ppermute(value, "section", pairs)


def local(state_coef, embed_terms, norm_gain, w_query, w_keyval, w_out, basis, doc_lengths):
    w_q, w_kv, w_o = w_query[0], w_keyval[0], w_out[0]
    depth = embed_terms.shape[-1]
    width = depth * PARTS
    shape = jax.ShapeDtypeStruct
    flops, moved = 2 * ROWS * depth * (RANK + WIDTH), 5 * MIB

    def finish(step, sent, tables, rows):
        return call(
            functools.partial(finish_kernel, width, step), f"finish{step}",
            shape((PARTS, rows, HEAD), BF16), [VMEM] * 2,
            16 * rows * HEAD, 3 * MIB, (exchange(sent), tables),
        )

    coef0 = state_coef[0]
    args = (doc_lengths, basis, w_o, coef0, embed_terms, norm_gain, w_q, w_kv)
    held = [pltpu.VMEM(arg.shape, BF16) for arg in args]
    held[0] = pltpu.SMEM(doc_lengths.shape, jnp.int32)
    held[4] = pltpu.VMEM((ROWS, depth), BF16)
    sent0, tables = call(
        project0_kernel, "project0",
        (pltpu.VMEM((PARTS, MIXED_ROWS + TAIL, HEAD), BF16), pltpu.VMEM((4, OWN, HEAD), F32)),
        [ANY] * len(args), 2 * flops, moved, args,
        held + [pltpu.SemaphoreType.DMA((len(args),))], (VMEM, VMEM), LIMIT0,
    )
    mixed = exchange(finish(0, sent0, tables, MIXED_ROWS))
    attended = pltpu.VMEM((ROWS, WIDTH_Q), BF16)
    attend_flops = 4 * ROWS * (ROWS * WIDTH_Q + RANK * RANK)
    step0 = (mixed, coef0, doc_lengths)
    boundary_even = call(
        functools.partial(first_kernel, 0), "attend0_even", shape((ROWS, RANK), BF16),
        [VMEM] * 2 + [SMEM], attend_flops, 3 * MIB, step0, [attended],
    )
    coef1_odd = hop(boundary_even, 0)
    boundary_odd = call(
        functools.partial(first_kernel, 1), "attend0_odd", shape((ROWS, RANK), BF16),
        [VMEM] * 2 + [SMEM], attend_flops, 3 * MIB, step0, [attended],
    )
    coef1 = (hop(boundary_odd, 1), coef1_odd)
    args = (*coef1, norm_gain, basis, embed_terms, w_q, w_kv)
    sent1 = call(
        project1_kernel, "project1", shape((PARTS, QKV_ROWS + TAIL, HEAD), BF16),
        [VMEM] * len(args), flops, moved, args,
    )
    heads = exchange(finish(1, sent1, tables, QKV_ROWS))
    both = call(
        second_kernel, "attend1", shape((2, ROWS, RANK), BF16), [VMEM] * 6 + [SMEM],
        attend_flops, 4 * MIB,
        (heads, mixed, *coef1, boundary_odd, boundary_even, doc_lengths),
        [attended, pltpu.VMEM((2, ROWS, RANK), BF16), pltpu.SemaphoreType.DMA((3,))], HBM,
    )
    return both[None]


def solution(mesh):
    return jax.shard_map(
        local,
        mesh=mesh,
        in_specs=(
            P("section", None, None),
            P("section", None, None, "tensor"),
            P("section", "tensor"),
            P("section", "tensor", None),
            P("section", "tensor", None),
            P("section", None, "tensor"),
            P("tensor", None),
            P("section", None, None),
        ),
        out_specs=P("section", None, None, None),
        check_vma=False,
    )
```

time: 423 us -> 102 us (0.24)
  the two profiles are of different devices: /device:TPU:2 before, /device:TPU:104 now
where the time goes in v1:
time: 102 us
  blocking collectives  81.7 us (80%)
  Pallas kernels  12.3 us (12%)
  starting transfers between devices  6.35 us (6%)
  waiting for transfers between devices  1.31 us (1%)
    all_to_all x4, blocking collectives, exchange(): return lax.all_to_all(blocks, 'tensor', 0, 0)  81.7 us
    pallas_call x7, Pallas kernels, call(): pl.pallas_call(body, name=name, out_shape=out_shape, in_specs=in_specs, o...  12.3 us
    ppermute x2, starting transfers between devices, hop(): return lax.ppermute(value, 'section', pairs)  6.35 us
  transfers between devices with their start and end apart: 2, of which 2 were waited for; matrix products, arithmetic and copies ran while one was open for 0% of the time, Pallas kernels for 2%

profile of v1, /device:TPU:104, one launch (start us, length us, event | category | flops | bytes accessed | tf_op | source)
XLA Modules:
  0.0 101.8 jit_solution(6467131519182153474)
XLA Ops:
  0.0 4.6 %project0.1 = (bf16[8,720,128]{2,1,0:T(8,128)(2,1)S(1)}, f32[4,48,128]{2,1,0:T(8,128)S(1)}) custom-call(s32[1,2,4]{2,1,0:T(2,128)} %lengths.5, bf16[1024,512]{1,0:T(8,128)(2,1)} %basis.1, bf16[512,1024]{1,0:T(8,128)(2,1)} %bitcast.12, bf16[384,512]{1,0:T(8,128)(2,1)} %bitcast.9, bf16[1,2,384,1024]{3,2,1,0:T(8,128)(2,1)} %emb.1, bf16[1,1024]{1,0:T(2,128)(2,1)} %gain.1, ...), custom_call_target="tpu_custom_call" | custom-call | flops 2013265920 | bytes 5242880 | tf_op jit(solution)/shard_map/project0/pallas_call | solution.py:41
  4.6 27.4 %all_to_all.20.parts = bf16[8,720,128]{2,1,0:T(8,128)(2,1)S(1)} all-to-all(bf16[8,720,128]{2,1,0:T(8,128)(2,1)S(1)} %get-tuple-element.7), channel_id=1, replica_groups=mesh['section'=64,'tensor'=8] {'tensor'}, dimensions={0} | all-to-all | bytes 2949120 | tf_op jit(solution)/shard_map/all_to_all | solution.py:305
  32.0 0.3 finish0.1
  32.3 0.0 copy-start.5
  32.3 0.0 copy-start.6
  32.3 23.2 %all_to_all.21.gathered.mixed = bf16[8,704,128]{2,1,0:T(8,128)(2,1)S(1)} all-to-all(bf16[8,704,128]{2,1,0:T(8,128)(2,1)S(1)} %finish0.1), channel_id=1, replica_groups=mesh['section'=64,'tensor'=8] {'tensor'}, dimensions={0} | all-to-all | bytes 2883584 | tf_op jit(solution)/shard_map/all_to_all | solution.py:305
  55.5 0.0 copy-done.5
  55.5 0.0 copy-done.6
  55.5 0.0 copy-start.1
  55.5 0.0 copy-start.2
  55.5 0.6 attend0_odd.1.before_odd
  56.1 0.0 copy-start
  56.1 0.0 copy-start.3
  56.1 0.0 copy-start.4
  56.1 1.4 %collective-permute-start = (bf16[384,512]{1,0:T(8,128)(2,1)S(1)}, bf16[384,512]{1,0:T(8,128)(2,1)S(1)}, u32[]{:S(2)}, u32[]{:S(2)}) collective-permute-start(bf16[384,512]{1,0:T(8,128)(2,1)S(1)} %attend0_odd.1.before_odd), channel_id=1, source_target_pairs={{8,16},{24,32},{40,48},{56,64},{72,80},{88,96},{104,112},{120,128}... | collective-permute-start | bytes 1179656 | tf_op jit(solution)/shard_map/ppermute | solution.py:311
  57.5 2.2 %attend0_even.1.before_even = bf16[384,512]{1,0:T(8,128)(2,1)S(1)} custom-call(bf16[8,704,128]{2,1,0:T(8,128)(2,1)S(1)} %all_to_all.21.gathered.mixed, bf16[384,512]{1,0:T(8,128)(2,1)S(1)} %bitcast.11, s32[1,2,4]{2,1,0:T(2,128)S(1)} %copy-done.5), custom_call_target="tpu_custom_call" | custom-call | flops 704643072 | bytes 3145728 | tf_op jit(solution)/shard_map/attend0_even/pallas_call | solution.py:41
  59.8 4.9 %collective-permute-start.1 = (bf16[384,512]{1,0:T(8,128)(2,1)S(1)}, bf16[384,512]{1,0:T(8,128)(2,1)S(1)}, u32[]{:S(2)}, u32[]{:S(2)}) collective-permute-start(bf16[384,512]{1,0:T(8,128)(2,1)S(1)} %attend0_even.1.before_even), channel_id=1, source_target_pairs={{0,8},{16,24},{32,40},{48,56},{64,72},{80,88},{96,104},{112,120},{... | collective-permute-start | bytes 1179656 | tf_op jit(solution)/shard_map/ppermute | solution.py:311
  64.7 0.6 collective-permute-done.coef_a
  65.3 0.7 collective-permute-done.1.coef_b
  66.0 0.0 copy-done.1
  66.0 0.0 copy-done.2
  66.0 0.0 copy-done
  66.0 0.0 copy-done.3
  66.0 0.0 copy-done.4
  66.0 1.4 %project1.1 = bf16[8,304,128]{2,1,0:T(8,128)(2,1)S(1)} custom-call(bf16[384,512]{1,0:T(8,128)(2,1)S(1)} %collective-permute-done.coef_a, bf16[384,512]{1,0:T(8,128)(2,1)S(1)} %collective-permute-done.1.coef_b, bf16[1,1024]{1,0:T(2,128)(2,1)S(1)} %copy-done.4, bf16[1024,512]{1,0:T(8,128)(2,1)S(1)} %copy-done.1, bf16[1,2,384,1024]{3,2,1,0:T(8,128)(2,1)S(1)} %copy-done, ...), custom_call_target="tpu_custom_call" | custom-call | flops 1006632960 | bytes 5242880 | tf_op jit(solution)/shard_map/project1/pallas_call | solution.py:41
  67.4 16.1 %all_to_all.22.parts = bf16[8,304,128]{2,1,0:T(8,128)(2,1)S(1)} all-to-all(bf16[8,304,128]{2,1,0:T(8,128)(2,1)S(1)} %project1.1), channel_id=1, replica_groups=mesh['section'=64,'tensor'=8] {'tensor'}, dimensions={0} | all-to-all | bytes 1245184 | tf_op jit(solution)/shard_map/all_to_all | solution.py:305
  83.6 0.2 finish1.1
  83.8 15.0 %all_to_all.23.gathered = bf16[8,288,128]{2,1,0:T(8,128)(2,1)S(1)} all-to-all(bf16[8,288,128]{2,1,0:T(8,128)(2,1)S(1)} %finish1.1), channel_id=1, replica_groups=mesh['section'=64,'tensor'=8] {'tensor'}, dimensions={0} | all-to-all | bytes 1179648 | tf_op jit(solution)/shard_map/all_to_all | solution.py:305
  98.8 3.0 %attend1.1 = bf16[2,384,512]{2,1,0:T(8,128)(2,1)} custom-call(bf16[8,288,128]{2,1,0:T(8,128)(2,1)S(1)} %all_to_all.23.gathered, bf16[8,704,128]{2,1,0:T(8,128)(2,1)S(1)} %all_to_all.21.gathered.mixed, bf16[384,512]{1,0:T(8,128)(2,1)S(1)} %collective-permute-done.coef_a, bf16[384,512]{1,0:T(8,128)(2,1)S(1)} %collective-permute-done.1.coef_b, ...), custom_call_target="tpu_custom_call" | custom-call | flops 704643072 | bytes 4194304 | tf_op jit(solution)/shard_map/attend1/pallas_call | solution.py:41
Async XLA Ops:
  32.3 23.2 %copy-start.5 = (s32[1,2,4]{2,1,0:T(2,128)S(1)}, s32[1,2,4]{2,1,0:T(2,128)}, u32[]{:S(2)}) copy-start(s32[1,2,4]{2,1,0:T(2,128)} %lengths.5) | copy-start | bytes 100
  32.3 23.2 %copy-start.6 = (bf16[1,384,512]{2,1,0:T(8,128)(2,1)S(1)}, bf16[1,384,512]{2,1,0:T(8,128)(2,1)}, u32[]{:S(2)}) copy-start(bf16[1,384,512]{2,1,0:T(8,128)(2,1)} %param.8) | copy-start | bytes 1179652
  55.5 10.5 %copy-start.1 = (bf16[1024,512]{1,0:T(8,128)(2,1)S(1)}, bf16[1024,512]{1,0:T(8,128)(2,1)}, u32[]{:S(2)}) copy-start(bf16[1024,512]{1,0:T(8,128)(2,1)} %basis.1) | copy-start | bytes 3145732
  55.5 10.5 %copy-start.2 = (bf16[1,1024,512]{2,1,0:T(8,128)(2,1)S(1)}, bf16[1,1024,512]{2,1,0:T(8,128)(2,1)}, u32[]{:S(2)}) copy-start(bf16[1,1024,512]{2,1,0:T(8,128)(2,1)} %param.11) | copy-start | bytes 3145732
  56.1 10.0 %copy-start = (bf16[1,2,384,1024]{3,2,1,0:T(8,128)(2,1)S(1)}, bf16[1,2,384,1024]{3,2,1,0:T(8,128)(2,1)}, u32[]{:S(2)}) copy-start(bf16[1,2,384,1024]{3,2,1,0:T(8,128)(2,1)} %emb.1) | copy-start | bytes 4718596
  56.1 9.9 %copy-start.3 = (bf16[1,1024,256]{2,1,0:T(8,128)(2,1)S(1)}, bf16[1,1024,256]{2,1,0:T(8,128)(2,1)}, u32[]{:S(2)}) copy-start(bf16[1,1024,256]{2,1,0:T(8,128)(2,1)} %param.12) | copy-start | bytes 1572868
  56.1 9.9 %copy-start.4 = (bf16[1,1024]{1,0:T(2,128)(2,1)S(1)}, bf16[1,1024]{1,0:T(2,128)(2,1)}, u32[]{:S(2)}) copy-start(bf16[1,1024]{1,0:T(2,128)(2,1)} %gain.1) | copy-start | bytes 6148
  56.1 9.2 %collective-permute-start = (bf16[384,512]{1,0:T(8,128)(2,1)S(1)}, bf16[384,512]{1,0:T(8,128)(2,1)S(1)}, u32[]{:S(2)}, u32[]{:S(2)}) collective-permute-start(bf16[384,512]{1,0:T(8,128)(2,1)S(1)} %attend0_odd.1.before_odd), channel_id=1, source_target_pairs={{8,16},{24,32},{40,48},{56,64},{72,80},{88,96},{104,112},{120,128}... | collective-permute-start | bytes 1179656 | tf_op jit(solution)/shard_map/ppermute | solution.py:311
  59.8 6.2 %collective-permute-start.1 = (bf16[384,512]{1,0:T(8,128)(2,1)S(1)}, bf16[384,512]{1,0:T(8,128)(2,1)S(1)}, u32[]{:S(2)}, u32[]{:S(2)}) collective-permute-start(bf16[384,512]{1,0:T(8,128)(2,1)S(1)} %attend0_even.1.before_even), channel_id=1, source_target_pairs={{0,8},{16,24},{32,40},{48,56},{64,72},{80,88},{96,104},{112,120},{... | collective-permute-start | bytes 1179656 | tf_op jit(solution)/shard_map/ppermute | solution.py:311

commit v2 on v1

--- a/solution.py
+++ b/solution.py
@@ -263,42 +263,45 @@
     ]
 
 
-def first_kernel(parity, gathered, coef, lengths, out, attended):
+def first_kernel(parity, gathered, coef, lengths_in, out, attended, lengths, sem):
     @pl.when(lax.axis_index("section") % 2 == parity)
     def _():
+        copy = pltpu.make_async_copy(lengths_in, lengths, sem)
+        copy.start()
+        copy.wait()
         attention(gathered, [lengths[0, 0, i] for i in range(3)], attended)
         for panel, value in enumerate(boundary_panels(coef, attended, gathered)):
             out[:, panel * PANEL : (panel + 1) * PANEL] = value
 
 
 def second_kernel(
-    gathered, mixed, coef_a, coef_b, before_odd, before_even, lengths, out, attended, buffer, sems
+    gathered, mixed, coef_a, coef_b, before_odd, before_even, lengths_in, out,
+    attended, buffer, lengths, sems,
 ):
+    lengths_copy = pltpu.make_async_copy(lengths_in, lengths, sems.at[3])
+    lengths_copy.start()
     odd = lax.axis_index("section") % 2 == 1
-
-    @pl.when(odd)
-    def _():
-        buffer[0] = before_odd[...]
-
-    @pl.when(jnp.logical_not(odd))
-    def _():
-        buffer[0] = before_even[...]
-
-    copies = [pltpu.make_async_copy(buffer.at[0], out.at[0], sems.at[0])]
-    copies[0].start()
+    from_odd = pltpu.make_async_copy(before_odd, out.at[0], sems.at[0])
+    from_even = pltpu.make_async_copy(before_even, out.at[0], sems.at[4])
+    pl.when(odd)(from_odd.start)
+    pl.when(jnp.logical_not(odd))(from_even.start)
+    copies = []
+    lengths_copy.wait()
     coef = coef_a[...] + coef_b[...]
     attention(gathered, [lengths[0, 1, i] for i in range(3)], attended)
     for panel, value in enumerate(boundary_panels(coef, attended, mixed)):
         columns = pl.ds(panel * PANEL, PANEL)
-        buffer[1, :, columns] = value
+        buffer[:, columns] = value
         copies.append(
             pltpu.make_async_copy(
-                buffer.at[1, :, columns], out.at[1, :, columns], sems.at[1 + panel]
+                buffer.at[:, columns], out.at[1, :, columns], sems.at[1 + panel]
             )
         )
         copies[-1].start()
     for copy in copies:
         copy.wait()
+    pl.when(odd)(from_odd.wait)
+    pl.when(jnp.logical_not(odd))(from_even.wait)
 
 
 def exchange(blocks):
@@ -338,16 +341,19 @@
     )
     mixed = exchange(finish(0, sent0, tables, MIXED_ROWS))
     attended = pltpu.VMEM((ROWS, WIDTH_Q), BF16)
+    lengths = pltpu.SMEM(doc_lengths.shape, jnp.int32)
     attend_flops = 4 * ROWS * (ROWS * WIDTH_Q + RANK * RANK)
     step0 = (mixed, coef0, doc_lengths)
     boundary_even = call(
         functools.partial(first_kernel, 0), "attend0_even", shape((ROWS, RANK), BF16),
-        [VMEM] * 2 + [SMEM], attend_flops, 3 * MIB, step0, [attended],
+        [VMEM] * 2 + [ANY], attend_flops, 3 * MIB, step0,
+        [attended, lengths, pltpu.SemaphoreType.DMA(())],
     )
     coef1_odd = hop(boundary_even, 0)
     boundary_odd = call(
         functools.partial(first_kernel, 1), "attend0_odd", shape((ROWS, RANK), BF16),
-        [VMEM] * 2 + [SMEM], attend_flops, 3 * MIB, step0, [attended],
+        [VMEM] * 2 + [ANY], attend_flops, 3 * MIB, step0,
+        [attended, lengths, pltpu.SemaphoreType.DMA(())],
     )
     coef1 = (hop(boundary_odd, 1), coef1_odd)
     args = (*coef1, norm_gain, basis, embed_terms, w_q, w_kv)
@@ -357,10 +363,10 @@
     )
     heads = exchange(finish(1, sent1, tables, QKV_ROWS))
     both = call(
-        second_kernel, "attend1", shape((2, ROWS, RANK), BF16), [VMEM] * 6 + [SMEM],
+        second_kernel, "attend1", shape((2, ROWS, RANK), BF16), [VMEM] * 6 + [ANY],
         attend_flops, 4 * MIB,
         (heads, mixed, *coef1, boundary_odd, boundary_even, doc_lengths),
-        [attended, pltpu.VMEM((2, ROWS, RANK), BF16), pltpu.SemaphoreType.DMA((3,))], HBM,
+        [attended, pltpu.VMEM((ROWS, RANK), BF16), lengths, pltpu.SemaphoreType.DMA((5,))], HBM,
     )
     return both[None]
 

time: 102 us -> 102 us (level)
  no operation moved by 1% of the time
where the time goes in v2:
time: 102 us; the launch traced here: 101 us
  blocking collectives  82.2 us (81%)
  Pallas kernels  11.7 us (11%)
  starting transfers between devices  5.93 us (6%)
  waiting for transfers between devices  1.31 us (1%)
    all_to_all x4, blocking collectives, exchange(): return lax.all_to_all(blocks, 'tensor', 0, 0)  82.2 us
    pallas_call x7, Pallas kernels, call(): pl.pallas_call(body, name=name, out_shape=out_shape, in_specs=in_specs, o...  11.7 us
    ppermute x2, starting transfers between devices, hop(): return lax.ppermute(value, 'section', pairs)  5.93 us
  transfers between devices with their start and end apart: 2, of which 2 were waited for; matrix products, arithmetic and copies ran while one was open for 0% of the time, Pallas kernels for 2%

profile of v2, /device:TPU:104, one launch (start us, length us, event | category | flops | bytes accessed | tf_op | source)
XLA Modules:
  0.0 101.3 jit_solution(17934270833858557961)
XLA Ops:
  0.0 4.6 %project0.1 = (bf16[8,720,128]{2,1,0:T(8,128)(2,1)S(1)}, f32[4,48,128]{2,1,0:T(8,128)S(1)}) custom-call(s32[1,2,4]{2,1,0:T(2,128)} %lengths_in.7, bf16[1024,512]{1,0:T(8,128)(2,1)} %basis.1, bf16[512,1024]{1,0:T(8,128)(2,1)} %bitcast.12, bf16[384,512]{1,0:T(8,128)(2,1)} %bitcast.9, bf16[1,2,384,1024]{3,2,1,0:T(8,128)(2,1)} %emb.1, bf16[1,1024]{1,0:T(2,128)(2,1)} %gain.1, ...), custom_call_target="tpu_custom_call" | custom-call | flops 2013265920 | bytes 5242880 | tf_op jit(solution)/shard_map/project0/pallas_call | solution.py:41
  4.6 27.4 %all_to_all.20.parts = bf16[8,720,128]{2,1,0:T(8,128)(2,1)S(1)} all-to-all(bf16[8,720,128]{2,1,0:T(8,128)(2,1)S(1)} %get-tuple-element.7), channel_id=1, replica_groups=mesh['section'=64,'tensor'=8] {'tensor'}, dimensions={0} | all-to-all | bytes 2949120 | tf_op jit(solution)/shard_map/all_to_all | solution.py:308
  32.0 0.3 finish0.1
  32.3 0.0 copy-start.5
  32.3 0.0 copy-start.6
  32.3 23.2 %all_to_all.21.gathered.mixed = bf16[8,704,128]{2,1,0:T(8,128)(2,1)S(1)} all-to-all(bf16[8,704,128]{2,1,0:T(8,128)(2,1)S(1)} %finish0.1), channel_id=1, replica_groups=mesh['section'=64,'tensor'=8] {'tensor'}, dimensions={0} | all-to-all | bytes 2883584 | tf_op jit(solution)/shard_map/all_to_all | solution.py:308
  55.5 0.0 copy-done.5
  55.5 0.0 copy-done.6
  55.5 0.0 copy-start.1
  55.5 0.0 copy-start.2
  55.5 0.0 copy-start
  55.5 0.0 copy-start.3
  55.5 0.0 copy-start.4
  55.6 1.6 %collective-permute-start = (bf16[384,512]{1,0:T(8,128)(2,1)S(1)}, bf16[384,512]{1,0:T(8,128)(2,1)S(1)}, u32[]{:S(2)}, u32[]{:S(2)}) collective-permute-start(bf16[384,512]{1,0:T(8,128)(2,1)S(1)} %attend0_odd.1.before_odd), channel_id=1, source_target_pairs={{8,16},{24,32},{40,48},{56,64},{72,80},{88,96},{104,112},{120,128}... | collective-permute-start | bytes 1179656 | tf_op jit(solution)/shard_map/ppermute | solution.py:314
  57.1 2.2 %attend0_even.1.before_even = bf16[384,512]{1,0:T(8,128)(2,1)S(1)} custom-call(bf16[8,704,128]{2,1,0:T(8,128)(2,1)S(1)} %all_to_all.21.gathered.mixed, bf16[384,512]{1,0:T(8,128)(2,1)S(1)} %bitcast.11, s32[1,2,4]{2,1,0:T(2,128)S(1)} %copy-done.5), custom_call_target="tpu_custom_call" | custom-call | flops 704643072 | bytes 3145728 | tf_op jit(solution)/shard_map/attend0_even/pallas_call | solution.py:41
  59.4 4.4 %collective-permute-start.1 = (bf16[384,512]{1,0:T(8,128)(2,1)S(1)}, bf16[384,512]{1,0:T(8,128)(2,1)S(1)}, u32[]{:S(2)}, u32[]{:S(2)}) collective-permute-start(bf16[384,512]{1,0:T(8,128)(2,1)S(1)} %attend0_even.1.before_even), channel_id=1, source_target_pairs={{0,8},{16,24},{32,40},{48,56},{64,72},{80,88},{96,104},{112,120},{... | collective-permute-start | bytes 1179656 | tf_op jit(solution)/shard_map/ppermute | solution.py:314
  63.7 1.2 %collective-permute-done.coef_a = bf16[384,512]{1,0:T(8,128)(2,1)S(1)} collective-permute-done((bf16[384,512]{1,0:T(8,128)(2,1)S(1)}, bf16[384,512]{1,0:T(8,128)(2,1)S(1)}, u32[]{:S(2)}, u32[]{:S(2)}) %collective-permute-start) | collective-permute-done | bytes 393248 | tf_op jit(solution)/shard_map/ppermute | solution.py:314
  64.9 0.1 collective-permute-done.1.coef_b
  65.1 0.0 copy-done.1
  65.1 0.0 copy-done.2
  65.1 0.0 copy-done
  65.1 0.0 copy-done.3
  65.1 0.0 copy-done.4
  65.1 1.4 %project1.1 = bf16[8,304,128]{2,1,0:T(8,128)(2,1)S(1)} custom-call(bf16[384,512]{1,0:T(8,128)(2,1)S(1)} %collective-permute-done.coef_a, bf16[384,512]{1,0:T(8,128)(2,1)S(1)} %collective-permute-done.1.coef_b, bf16[1,1024]{1,0:T(2,128)(2,1)S(1)} %copy-done.4, bf16[1024,512]{1,0:T(8,128)(2,1)S(1)} %copy-done.1, bf16[1,2,384,1024]{3,2,1,0:T(8,128)(2,1)S(1)} %copy-done, ...), custom_call_target="tpu_custom_call" | custom-call | flops 1006632960 | bytes 5242880 | tf_op jit(solution)/shard_map/project1/pallas_call | solution.py:41
  66.5 16.0 %all_to_all.22.parts = bf16[8,304,128]{2,1,0:T(8,128)(2,1)S(1)} all-to-all(bf16[8,304,128]{2,1,0:T(8,128)(2,1)S(1)} %project1.1), channel_id=1, replica_groups=mesh['section'=64,'tensor'=8] {'tensor'}, dimensions={0} | all-to-all | bytes 1245184 | tf_op jit(solution)/shard_map/all_to_all | solution.py:308
  82.5 0.2 finish1.1
  82.7 15.6 %all_to_all.23.gathered = bf16[8,288,128]{2,1,0:T(8,128)(2,1)S(1)} all-to-all(bf16[8,288,128]{2,1,0:T(8,128)(2,1)S(1)} %finish1.1), channel_id=1, replica_groups=mesh['section'=64,'tensor'=8] {'tensor'}, dimensions={0} | all-to-all | bytes 1179648 | tf_op jit(solution)/shard_map/all_to_all | solution.py:308
  98.3 3.0 %attend1.1 = bf16[2,384,512]{2,1,0:T(8,128)(2,1)} custom-call(bf16[8,288,128]{2,1,0:T(8,128)(2,1)S(1)} %all_to_all.23.gathered, bf16[8,704,128]{2,1,0:T(8,128)(2,1)S(1)} %all_to_all.21.gathered.mixed, bf16[384,512]{1,0:T(8,128)(2,1)S(1)} %collective-permute-done.coef_a, bf16[384,512]{1,0:T(8,128)(2,1)S(1)} %collective-permute-done.1.coef_b, ...), custom_call_target="tpu_custom_call" | custom-call | flops 704643072 | bytes 4194304 | tf_op jit(solution)/shard_map/attend1/pallas_call | solution.py:41
  (1 shorter events, 0.0 us)
Async XLA Ops:
  32.3 23.2 %copy-start.5 = (s32[1,2,4]{2,1,0:T(2,128)S(1)}, s32[1,2,4]{2,1,0:T(2,128)}, u32[]{:S(2)}) copy-start(s32[1,2,4]{2,1,0:T(2,128)} %lengths_in.7) | copy-start | bytes 100
  32.3 23.2 %copy-start.6 = (bf16[1,384,512]{2,1,0:T(8,128)(2,1)S(1)}, bf16[1,384,512]{2,1,0:T(8,128)(2,1)}, u32[]{:S(2)}) copy-start(bf16[1,384,512]{2,1,0:T(8,128)(2,1)} %param.8) | copy-start | bytes 1179652
  55.5 9.6 %copy-start.1 = (bf16[1024,512]{1,0:T(8,128)(2,1)S(1)}, bf16[1024,512]{1,0:T(8,128)(2,1)}, u32[]{:S(2)}) copy-start(bf16[1024,512]{1,0:T(8,128)(2,1)} %basis.1) | copy-start | bytes 3145732
  55.5 9.6 %copy-start.2 = (bf16[1,1024,512]{2,1,0:T(8,128)(2,1)S(1)}, bf16[1,1024,512]{2,1,0:T(8,128)(2,1)}, u32[]{:S(2)}) copy-start(bf16[1,1024,512]{2,1,0:T(8,128)(2,1)} %param.11) | copy-start | bytes 3145732
  55.5 9.6 %copy-start = (bf16[1,2,384,1024]{3,2,1,0:T(8,128)(2,1)S(1)}, bf16[1,2,384,1024]{3,2,1,0:T(8,128)(2,1)}, u32[]{:S(2)}) copy-start(bf16[1,2,384,1024]{3,2,1,0:T(8,128)(2,1)} %emb.1) | copy-start | bytes 4718596
  55.5 9.5 %copy-start.3 = (bf16[1,1024,256]{2,1,0:T(8,128)(2,1)S(1)}, bf16[1,1024,256]{2,1,0:T(8,128)(2,1)}, u32[]{:S(2)}) copy-start(bf16[1,1024,256]{2,1,0:T(8,128)(2,1)} %param.12) | copy-start | bytes 1572868
  55.5 9.5 %copy-start.4 = (bf16[1,1024]{1,0:T(2,128)(2,1)S(1)}, bf16[1,1024]{1,0:T(2,128)(2,1)}, u32[]{:S(2)}) copy-start(bf16[1,1024]{1,0:T(2,128)(2,1)} %gain.1) | copy-start | bytes 6148
  55.6 9.4 %collective-permute-start = (bf16[384,512]{1,0:T(8,128)(2,1)S(1)}, bf16[384,512]{1,0:T(8,128)(2,1)S(1)}, u32[]{:S(2)}, u32[]{:S(2)}) collective-permute-start(bf16[384,512]{1,0:T(8,128)(2,1)S(1)} %attend0_odd.1.before_odd), channel_id=1, source_target_pairs={{8,16},{24,32},{40,48},{56,64},{72,80},{88,96},{104,112},{120,128}... | collective-permute-start | bytes 1179656 | tf_op jit(solution)/shard_map/ppermute | solution.py:314
  59.4 5.7 %collective-permute-start.1 = (bf16[384,512]{1,0:T(8,128)(2,1)S(1)}, bf16[384,512]{1,0:T(8,128)(2,1)S(1)}, u32[]{:S(2)}, u32[]{:S(2)}) collective-permute-start(bf16[384,512]{1,0:T(8,128)(2,1)S(1)} %attend0_even.1.before_even), channel_id=1, source_target_pairs={{0,8},{16,24},{32,40},{48,56},{64,72},{80,88},{96,104},{112,120},{... | collective-permute-start | bytes 1179656 | tf_op jit(solution)/shard_map/ppermute | solution.py:314

commit v3 on v2

--- a/solution.py
+++ b/solution.py
@@ -241,15 +241,14 @@
         begin = jnp.where(row >= first, first, 0)
         begin = jnp.where(row >= second, second, begin)
         begin = jnp.where(row >= third, third, begin)
-        allowed = (column >= begin) & (column <= row)
-        scores = dot_t(queries, keys) * HEAD ** (-0.5)
+        bias = jnp.where((column >= begin) & (column <= row), 0.0, -1e30)
+        scores = dot_t(queries, keys).reshape(GROUP, HEAD, count) * HEAD ** (-0.5) + bias[None]
+        scores = scores.reshape(GROUP * HEAD, count)
+        weights = jnp.exp(scores - jnp.max(scores, axis=-1, keepdims=True)).astype(BF16)
+        summed = dot(weights, values)
+        result = (summed[:, :HEAD] / summed[:, HEAD:]).astype(BF16)
         for h in range(GROUP):
-            own = jnp.where(allowed, scores[h * HEAD : (h + 1) * HEAD], -1e30)
-            weights = jnp.exp(own - jnp.max(own, axis=-1, keepdims=True)).astype(BF16)
-            summed = dot(weights, values)
-            attended[at:count, h * HEAD : (h + 1) * HEAD] = (
-                summed[:, :HEAD] / summed[:, HEAD:]
-            ).astype(BF16)
+            attended[at:count, h * HEAD : (h + 1) * HEAD] = result[h * HEAD : (h + 1) * HEAD]
 
 
 def boundary_panels(coef, attended, mixed):

time: 102 us -> 102 us (level)
  no operation moved by 1% of the time
where the time goes in v3:
time: 102 us; the launch traced here: 101 us
  blocking collectives  82.2 us (81%)
  Pallas kernels  12.1 us (12%)
  starting transfers between devices  5.71 us (6%)
  waiting for transfers between devices  1.31 us (1%)
    all_to_all x4, blocking collectives, exchange(): return lax.all_to_all(blocks, 'tensor', 0, 0)  82.2 us
    pallas_call x7, Pallas kernels, call(): pl.pallas_call(body, name=name, out_shape=out_shape, in_specs=in_specs, o...  12.1 us
    ppermute x2, starting transfers between devices, hop(): return lax.ppermute(value, 'section', pairs)  5.71 us
  transfers between devices with their start and end apart: 2, of which 2 were waited for; matrix products, arithmetic and copies ran while one was open for 0% of the time, Pallas kernels for 2%

profile of v3, /device:TPU:104, one launch (start us, length us, event | category | flops | bytes accessed | tf_op | source)
XLA Modules:
  0.0 101.5 jit_solution(13936919742903469809)
XLA Ops:
  0.0 4.6 %project0.1 = (bf16[8,720,128]{2,1,0:T(8,128)(2,1)S(1)}, f32[4,48,128]{2,1,0:T(8,128)S(1)}) custom-call(s32[1,2,4]{2,1,0:T(2,128)} %lengths_in.7, bf16[1024,512]{1,0:T(8,128)(2,1)} %basis.1, bf16[512,1024]{1,0:T(8,128)(2,1)} %bitcast.12, bf16[384,512]{1,0:T(8,128)(2,1)} %bitcast.9, bf16[1,2,384,1024]{3,2,1,0:T(8,128)(2,1)} %emb.1, bf16[1,1024]{1,0:T(2,128)(2,1)} %gain.1, ...), custom_call_target="tpu_custom_call" | custom-call | flops 2013265920 | bytes 5242880 | tf_op jit(solution)/shard_map/project0/pallas_call | solution.py:41
  4.6 27.4 %all_to_all.20.parts = bf16[8,720,128]{2,1,0:T(8,128)(2,1)S(1)} all-to-all(bf16[8,720,128]{2,1,0:T(8,128)(2,1)S(1)} %get-tuple-element.7), channel_id=1, replica_groups=mesh['section'=64,'tensor'=8] {'tensor'}, dimensions={0} | all-to-all | bytes 2949120 | tf_op jit(solution)/shard_map/all_to_all | solution.py:307
  32.0 0.3 finish0.1
  32.3 0.0 copy-start.5
  32.3 0.0 copy-start.6
  32.3 23.2 %all_to_all.21.gathered.mixed = bf16[8,704,128]{2,1,0:T(8,128)(2,1)S(1)} all-to-all(bf16[8,704,128]{2,1,0:T(8,128)(2,1)S(1)} %finish0.1), channel_id=1, replica_groups=mesh['section'=64,'tensor'=8] {'tensor'}, dimensions={0} | all-to-all | bytes 2883584 | tf_op jit(solution)/shard_map/all_to_all | solution.py:307
  55.5 0.0 copy-done.5
  55.5 0.0 copy-done.6
  55.5 0.0 copy-start.1
  55.5 0.0 copy-start.2
  55.5 0.0 copy-start
  55.5 0.0 copy-start.3
  55.5 0.0 copy-start.4
  55.6 1.6 %collective-permute-start = (bf16[384,512]{1,0:T(8,128)(2,1)S(1)}, bf16[384,512]{1,0:T(8,128)(2,1)S(1)}, u32[]{:S(2)}, u32[]{:S(2)}) collective-permute-start(bf16[384,512]{1,0:T(8,128)(2,1)S(1)} %attend0_odd.1.before_odd), channel_id=1, source_target_pairs={{8,16},{24,32},{40,48},{56,64},{72,80},{88,96},{104,112},{120,128}... | collective-permute-start | bytes 1179656 | tf_op jit(solution)/shard_map/ppermute | solution.py:313
  57.1 2.5 %attend0_even.1.before_even = bf16[384,512]{1,0:T(8,128)(2,1)S(1)} custom-call(bf16[8,704,128]{2,1,0:T(8,128)(2,1)S(1)} %all_to_all.21.gathered.mixed, bf16[384,512]{1,0:T(8,128)(2,1)S(1)} %bitcast.11, s32[1,2,4]{2,1,0:T(2,128)S(1)} %copy-done.5), custom_call_target="tpu_custom_call" | custom-call | flops 704643072 | bytes 3145728 | tf_op jit(solution)/shard_map/attend0_even/pallas_call | solution.py:41
  59.6 4.2 %collective-permute-start.1 = (bf16[384,512]{1,0:T(8,128)(2,1)S(1)}, bf16[384,512]{1,0:T(8,128)(2,1)S(1)}, u32[]{:S(2)}, u32[]{:S(2)}) collective-permute-start(bf16[384,512]{1,0:T(8,128)(2,1)S(1)} %attend0_even.1.before_even), channel_id=1, source_target_pairs={{0,8},{16,24},{32,40},{48,56},{64,72},{80,88},{96,104},{112,120},{... | collective-permute-start | bytes 1179656 | tf_op jit(solution)/shard_map/ppermute | solution.py:313
  63.7 1.2 %collective-permute-done.coef_a = bf16[384,512]{1,0:T(8,128)(2,1)S(1)} collective-permute-done((bf16[384,512]{1,0:T(8,128)(2,1)S(1)}, bf16[384,512]{1,0:T(8,128)(2,1)S(1)}, u32[]{:S(2)}, u32[]{:S(2)}) %collective-permute-start) | collective-permute-done | bytes 393248 | tf_op jit(solution)/shard_map/ppermute | solution.py:313
  64.9 0.1 collective-permute-done.1.coef_b
  65.1 0.0 copy-done.1
  65.1 0.0 copy-done.2
  65.1 0.0 copy-done
  65.1 0.0 copy-done.3
  65.1 0.0 copy-done.4
  65.1 1.4 %project1.1 = bf16[8,304,128]{2,1,0:T(8,128)(2,1)S(1)} custom-call(bf16[384,512]{1,0:T(8,128)(2,1)S(1)} %collective-permute-done.coef_a, bf16[384,512]{1,0:T(8,128)(2,1)S(1)} %collective-permute-done.1.coef_b, bf16[1,1024]{1,0:T(2,128)(2,1)S(1)} %copy-done.4, bf16[1024,512]{1,0:T(8,128)(2,1)S(1)} %copy-done.1, bf16[1,2,384,1024]{3,2,1,0:T(8,128)(2,1)S(1)} %copy-done, ...), custom_call_target="tpu_custom_call" | custom-call | flops 1006632960 | bytes 5242880 | tf_op jit(solution)/shard_map/project1/pallas_call | solution.py:41
  66.5 16.0 %all_to_all.22.parts = bf16[8,304,128]{2,1,0:T(8,128)(2,1)S(1)} all-to-all(bf16[8,304,128]{2,1,0:T(8,128)(2,1)S(1)} %project1.1), channel_id=1, replica_groups=mesh['section'=64,'tensor'=8] {'tensor'}, dimensions={0} | all-to-all | bytes 1245184 | tf_op jit(solution)/shard_map/all_to_all | solution.py:307
  82.5 0.2 finish1.1
  82.7 15.6 %all_to_all.23.gathered = bf16[8,288,128]{2,1,0:T(8,128)(2,1)S(1)} all-to-all(bf16[8,288,128]{2,1,0:T(8,128)(2,1)S(1)} %finish1.1), channel_id=1, replica_groups=mesh['section'=64,'tensor'=8] {'tensor'}, dimensions={0} | all-to-all | bytes 1179648 | tf_op jit(solution)/shard_map/all_to_all | solution.py:307
  98.3 3.2 %attend1.1 = bf16[2,384,512]{2,1,0:T(8,128)(2,1)} custom-call(bf16[8,288,128]{2,1,0:T(8,128)(2,1)S(1)} %all_to_all.23.gathered, bf16[8,704,128]{2,1,0:T(8,128)(2,1)S(1)} %all_to_all.21.gathered.mixed, bf16[384,512]{1,0:T(8,128)(2,1)S(1)} %collective-permute-done.coef_a, bf16[384,512]{1,0:T(8,128)(2,1)S(1)} %collective-permute-done.1.coef_b, ...), custom_call_target="tpu_custom_call" | custom-call | flops 704643072 | bytes 4194304 | tf_op jit(solution)/shard_map/attend1/pallas_call | solution.py:41
  (1 shorter events, 0.0 us)
Async XLA Ops:
  32.3 23.2 %copy-start.5 = (s32[1,2,4]{2,1,0:T(2,128)S(1)}, s32[1,2,4]{2,1,0:T(2,128)}, u32[]{:S(2)}) copy-start(s32[1,2,4]{2,1,0:T(2,128)} %lengths_in.7) | copy-start | bytes 100
  32.3 23.2 %copy-start.6 = (bf16[1,384,512]{2,1,0:T(8,128)(2,1)S(1)}, bf16[1,384,512]{2,1,0:T(8,128)(2,1)}, u32[]{:S(2)}) copy-start(bf16[1,384,512]{2,1,0:T(8,128)(2,1)} %param.8) | copy-start | bytes 1179652
  55.5 9.6 %copy-start.1 = (bf16[1024,512]{1,0:T(8,128)(2,1)S(1)}, bf16[1024,512]{1,0:T(8,128)(2,1)}, u32[]{:S(2)}) copy-start(bf16[1024,512]{1,0:T(8,128)(2,1)} %basis.1) | copy-start | bytes 3145732
  55.5 9.6 %copy-start.2 = (bf16[1,1024,512]{2,1,0:T(8,128)(2,1)S(1)}, bf16[1,1024,512]{2,1,0:T(8,128)(2,1)}, u32[]{:S(2)}) copy-start(bf16[1,1024,512]{2,1,0:T(8,128)(2,1)} %param.11) | copy-start | bytes 3145732
  55.5 9.6 %copy-start = (bf16[1,2,384,1024]{3,2,1,0:T(8,128)(2,1)S(1)}, bf16[1,2,384,1024]{3,2,1,0:T(8,128)(2,1)}, u32[]{:S(2)}) copy-start(bf16[1,2,384,1024]{3,2,1,0:T(8,128)(2,1)} %emb.1) | copy-start | bytes 4718596
  55.5 9.5 %copy-start.3 = (bf16[1,1024,256]{2,1,0:T(8,128)(2,1)S(1)}, bf16[1,1024,256]{2,1,0:T(8,128)(2,1)}, u32[]{:S(2)}) copy-start(bf16[1,1024,256]{2,1,0:T(8,128)(2,1)} %param.12) | copy-start | bytes 1572868
  55.5 9.5 %copy-start.4 = (bf16[1,1024]{1,0:T(2,128)(2,1)S(1)}, bf16[1,1024]{1,0:T(2,128)(2,1)}, u32[]{:S(2)}) copy-start(bf16[1,1024]{1,0:T(2,128)(2,1)} %gain.1) | copy-start | bytes 6148
  55.6 9.4 %collective-permute-start = (bf16[384,512]{1,0:T(8,128)(2,1)S(1)}, bf16[384,512]{1,0:T(8,128)(2,1)S(1)}, u32[]{:S(2)}, u32[]{:S(2)}) collective-permute-start(bf16[384,512]{1,0:T(8,128)(2,1)S(1)} %attend0_odd.1.before_odd), channel_id=1, source_target_pairs={{8,16},{24,32},{40,48},{56,64},{72,80},{88,96},{104,112},{120,128}... | collective-permute-start | bytes 1179656 | tf_op jit(solution)/shard_map/ppermute | solution.py:313
  59.6 5.5 %collective-permute-start.1 = (bf16[384,512]{1,0:T(8,128)(2,1)S(1)}, bf16[384,512]{1,0:T(8,128)(2,1)S(1)}, u32[]{:S(2)}, u32[]{:S(2)}) collective-permute-start(bf16[384,512]{1,0:T(8,128)(2,1)S(1)} %attend0_even.1.before_even), channel_id=1, source_target_pairs={{0,8},{16,24},{32,40},{48,56},{64,72},{80,88},{96,104},{112,120},{... | collective-permute-start | bytes 1179656 | tf_op jit(solution)/shard_map/ppermute | solution.py:313

commit v4 on v2

--- a/solution.py
+++ b/solution.py
@@ -252,13 +252,19 @@
             ).astype(BF16)
 
 
-def boundary_panels(coef, attended, mixed):
+def carried_panels(coef, mixed):
     first, second = coef[:, :PANEL], coef[:, PANEL:]
     upper, cross, lower = symmetric_blocks(mixed)
-    of_g = (dot(first, upper) + dot_t(second, cross), dot(first, cross) + dot(second, lower))
+    return dot(first, upper) + dot_t(second, cross), dot(first, cross) + dot(second, lower)
+
+
+def boundary_panels(carried, attended, mixed):
     columns = PANEL // HEAD
     return [
-        (of_g[panel] + dot(attended[...], unpack(mixed, M_AT + panel * columns * M_OWN, M_OWN, columns))).astype(BF16)
+        (
+            carried[panel]
+            + dot(attended[...], unpack(mixed, M_AT + panel * columns * M_OWN, M_OWN, columns))
+        ).astype(BF16)
         for panel in range(RANK // PANEL)
     ]
 
@@ -268,9 +274,10 @@
     def _():
         copy = pltpu.make_async_copy(lengths_in, lengths, sem)
         copy.start()
+        carried = carried_panels(coef[...], gathered)
         copy.wait()
         attention(gathered, [lengths[0, 0, i] for i in range(3)], attended)
-        for panel, value in enumerate(boundary_panels(coef, attended, gathered)):
+        for panel, value in enumerate(boundary_panels(carried, attended, gathered)):
             out[:, panel * PANEL : (panel + 1) * PANEL] = value
 
 
@@ -286,10 +293,10 @@
     pl.when(odd)(from_odd.start)
     pl.when(jnp.logical_not(odd))(from_even.start)
     copies = []
+    carried = carried_panels(coef_a[...] + coef_b[...], mixed)
     lengths_copy.wait()
-    coef = coef_a[...] + coef_b[...]
     attention(gathered, [lengths[0, 1, i] for i in range(3)], attended)
-    for panel, value in enumerate(boundary_panels(coef, attended, mixed)):
+    for panel, value in enumerate(boundary_panels(carried, attended, mixed)):
         columns = pl.ds(panel * PANEL, PANEL)
         buffer[:, columns] = value
         copies.append(

time: 102 us -> 101 us (level)
  no operation moved by 1% of the time
where the time goes in v4:
time: 101 us
  blocking collectives  82.2 us (81%)
  Pallas kernels  11.2 us (11%)
  starting transfers between devices  6.18 us (6%)
  waiting for transfers between devices  1.31 us (1%)
    all_to_all x4, blocking collectives, exchange(): return lax.all_to_all(blocks, 'tensor', 0, 0)  82.2 us
    pallas_call x7, Pallas kernels, call(): pl.pallas_call(body, name=name, out_shape=out_shape, in_specs=in_specs, o...  11.2 us
    ppermute x2, starting transfers between devices, hop(): return lax.ppermute(value, 'section', pairs)  6.18 us
  transfers between devices with their start and end apart: 2, of which 2 were waited for; matrix products, arithmetic and copies ran while one was open for 0% of the time, Pallas kernels for 2%

profile of v4, /device:TPU:104, one launch (start us, length us, event | category | flops | bytes accessed | tf_op | source)
XLA Modules:
  0.0 101.1 jit_solution(3289490457109667909)
XLA Ops:
  0.0 4.6 %project0.1 = (bf16[8,720,128]{2,1,0:T(8,128)(2,1)S(1)}, f32[4,48,128]{2,1,0:T(8,128)S(1)}) custom-call(s32[1,2,4]{2,1,0:T(2,128)} %lengths_in.7, bf16[1024,512]{1,0:T(8,128)(2,1)} %basis.1, bf16[512,1024]{1,0:T(8,128)(2,1)} %bitcast.12, bf16[384,512]{1,0:T(8,128)(2,1)} %bitcast.9, bf16[1,2,384,1024]{3,2,1,0:T(8,128)(2,1)} %emb.1, bf16[1,1024]{1,0:T(2,128)(2,1)} %gain.1, ...), custom_call_target="tpu_custom_call" | custom-call | flops 2013265920 | bytes 5242880 | tf_op jit(solution)/shard_map/project0/pallas_call | solution.py:41
  4.6 27.4 %all_to_all.20.parts = bf16[8,720,128]{2,1,0:T(8,128)(2,1)S(1)} all-to-all(bf16[8,720,128]{2,1,0:T(8,128)(2,1)S(1)} %get-tuple-element.7), channel_id=1, replica_groups=mesh['section'=64,'tensor'=8] {'tensor'}, dimensions={0} | all-to-all | bytes 2949120 | tf_op jit(solution)/shard_map/all_to_all | solution.py:315
  32.0 0.3 finish0.1
  32.3 0.0 copy-start.5
  32.3 0.0 copy-start.6
  32.3 23.2 %all_to_all.21.gathered.mixed = bf16[8,704,128]{2,1,0:T(8,128)(2,1)S(1)} all-to-all(bf16[8,704,128]{2,1,0:T(8,128)(2,1)S(1)} %finish0.1), channel_id=1, replica_groups=mesh['section'=64,'tensor'=8] {'tensor'}, dimensions={0} | all-to-all | bytes 2883584 | tf_op jit(solution)/shard_map/all_to_all | solution.py:315
  55.5 0.0 copy-done.5
  55.5 0.0 copy-done.6
  55.5 0.0 copy-start.1
  55.5 0.0 copy-start.2
  55.5 0.0 copy-start
  55.5 0.0 copy-start.3
  55.5 0.0 copy-start.4
  55.6 1.6 %collective-permute-start = (bf16[384,512]{1,0:T(8,128)(2,1)S(1)}, bf16[384,512]{1,0:T(8,128)(2,1)S(1)}, u32[]{:S(2)}, u32[]{:S(2)}) collective-permute-start(bf16[384,512]{1,0:T(8,128)(2,1)S(1)} %attend0_odd.1.before_odd), channel_id=1, source_target_pairs={{8,16},{24,32},{40,48},{56,64},{72,80},{88,96},{104,112},{120,128}... | collective-permute-start | bytes 1179656 | tf_op jit(solution)/shard_map/ppermute | solution.py:321
  57.1 2.0 %attend0_even.1.before_even = bf16[384,512]{1,0:T(8,128)(2,1)S(1)} custom-call(bf16[8,704,128]{2,1,0:T(8,128)(2,1)S(1)} %all_to_all.21.gathered.mixed, bf16[384,512]{1,0:T(8,128)(2,1)S(1)} %bitcast.11, s32[1,2,4]{2,1,0:T(2,128)S(1)} %copy-done.5), custom_call_target="tpu_custom_call" | custom-call | flops 704643072 | bytes 3145728 | tf_op jit(solution)/shard_map/attend0_even/pallas_call | solution.py:41
  59.1 4.6 %collective-permute-start.1 = (bf16[384,512]{1,0:T(8,128)(2,1)S(1)}, bf16[384,512]{1,0:T(8,128)(2,1)S(1)}, u32[]{:S(2)}, u32[]{:S(2)}) collective-permute-start(bf16[384,512]{1,0:T(8,128)(2,1)S(1)} %attend0_even.1.before_even), channel_id=1, source_target_pairs={{0,8},{16,24},{32,40},{48,56},{64,72},{80,88},{96,104},{112,120},{... | collective-permute-start | bytes 1179656 | tf_op jit(solution)/shard_map/ppermute | solution.py:321
  63.7 1.2 %collective-permute-done.coef_a = bf16[384,512]{1,0:T(8,128)(2,1)S(1)} collective-permute-done((bf16[384,512]{1,0:T(8,128)(2,1)S(1)}, bf16[384,512]{1,0:T(8,128)(2,1)S(1)}, u32[]{:S(2)}, u32[]{:S(2)}) %collective-permute-start) | collective-permute-done | bytes 393248 | tf_op jit(solution)/shard_map/ppermute | solution.py:321
  64.9 0.1 collective-permute-done.1.coef_b
  65.1 0.0 copy-done.1
  65.1 0.0 copy-done.2
  65.1 0.0 copy-done
  65.1 0.0 copy-done.3
  65.1 0.0 copy-done.4
  65.1 1.4 %project1.1 = bf16[8,304,128]{2,1,0:T(8,128)(2,1)S(1)} custom-call(bf16[384,512]{1,0:T(8,128)(2,1)S(1)} %collective-permute-done.coef_a, bf16[384,512]{1,0:T(8,128)(2,1)S(1)} %collective-permute-done.1.coef_b, bf16[1,1024]{1,0:T(2,128)(2,1)S(1)} %copy-done.4, bf16[1024,512]{1,0:T(8,128)(2,1)S(1)} %copy-done.1, bf16[1,2,384,1024]{3,2,1,0:T(8,128)(2,1)S(1)} %copy-done, ...), custom_call_target="tpu_custom_call" | custom-call | flops 1006632960 | bytes 5242880 | tf_op jit(solution)/shard_map/project1/pallas_call | solution.py:41
  66.5 16.0 %all_to_all.22.parts = bf16[8,304,128]{2,1,0:T(8,128)(2,1)S(1)} all-to-all(bf16[8,304,128]{2,1,0:T(8,128)(2,1)S(1)} %project1.1), channel_id=1, replica_groups=mesh['section'=64,'tensor'=8] {'tensor'}, dimensions={0} | all-to-all | bytes 1245184 | tf_op jit(solution)/shard_map/all_to_all | solution.py:315
  82.5 0.2 finish1.1
  82.7 15.6 %all_to_all.23.gathered = bf16[8,288,128]{2,1,0:T(8,128)(2,1)S(1)} all-to-all(bf16[8,288,128]{2,1,0:T(8,128)(2,1)S(1)} %finish1.1), channel_id=1, replica_groups=mesh['section'=64,'tensor'=8] {'tensor'}, dimensions={0} | all-to-all | bytes 1179648 | tf_op jit(solution)/shard_map/all_to_all | solution.py:315
  98.3 2.7 %attend1.1 = bf16[2,384,512]{2,1,0:T(8,128)(2,1)} custom-call(bf16[8,288,128]{2,1,0:T(8,128)(2,1)S(1)} %all_to_all.23.gathered, bf16[8,704,128]{2,1,0:T(8,128)(2,1)S(1)} %all_to_all.21.gathered.mixed, bf16[384,512]{1,0:T(8,128)(2,1)S(1)} %collective-permute-done.coef_a, bf16[384,512]{1,0:T(8,128)(2,1)S(1)} %collective-permute-done.1.coef_b, ...), custom_call_target="tpu_custom_call" | custom-call | flops 704643072 | bytes 4194304 | tf_op jit(solution)/shard_map/attend1/pallas_call | solution.py:41
  (1 shorter events, 0.0 us)
Async XLA Ops:
  32.3 23.2 %copy-start.5 = (s32[1,2,4]{2,1,0:T(2,128)S(1)}, s32[1,2,4]{2,1,0:T(2,128)}, u32[]{:S(2)}) copy-start(s32[1,2,4]{2,1,0:T(2,128)} %lengths_in.7) | copy-start | bytes 100
  32.3 23.2 %copy-start.6 = (bf16[1,384,512]{2,1,0:T(8,128)(2,1)S(1)}, bf16[1,384,512]{2,1,0:T(8,128)(2,1)}, u32[]{:S(2)}) copy-start(bf16[1,384,512]{2,1,0:T(8,128)(2,1)} %param.8) | copy-start | bytes 1179652
  55.5 9.6 %copy-start.1 = (bf16[1024,512]{1,0:T(8,128)(2,1)S(1)}, bf16[1024,512]{1,0:T(8,128)(2,1)}, u32[]{:S(2)}) copy-start(bf16[1024,512]{1,0:T(8,128)(2,1)} %basis.1) | copy-start | bytes 3145732
  55.5 9.6 %copy-start.2 = (bf16[1,1024,512]{2,1,0:T(8,128)(2,1)S(1)}, bf16[1,1024,512]{2,1,0:T(8,128)(2,1)}, u32[]{:S(2)}) copy-start(bf16[1,1024,512]{2,1,0:T(8,128)(2,1)} %param.11) | copy-start | bytes 3145732
  55.5 9.6 %copy-start = (bf16[1,2,384,1024]{3,2,1,0:T(8,128)(2,1)S(1)}, bf16[1,2,384,1024]{3,2,1,0:T(8,128)(2,1)}, u32[]{:S(2)}) copy-start(bf16[1,2,384,1024]{3,2,1,0:T(8,128)(2,1)} %emb.1) | copy-start | bytes 4718596
  55.5 9.5 %copy-start.3 = (bf16[1,1024,256]{2,1,0:T(8,128)(2,1)S(1)}, bf16[1,1024,256]{2,1,0:T(8,128)(2,1)}, u32[]{:S(2)}) copy-start(bf16[1,1024,256]{2,1,0:T(8,128)(2,1)} %param.12) | copy-start | bytes 1572868
  55.5 9.5 %copy-start.4 = (bf16[1,1024]{1,0:T(2,128)(2,1)S(1)}, bf16[1,1024]{1,0:T(2,128)(2,1)}, u32[]{:S(2)}) copy-start(bf16[1,1024]{1,0:T(2,128)(2,1)} %gain.1) | copy-start | bytes 6148
  55.6 9.4 %collective-permute-start = (bf16[384,512]{1,0:T(8,128)(2,1)S(1)}, bf16[384,512]{1,0:T(8,128)(2,1)S(1)}, u32[]{:S(2)}, u32[]{:S(2)}) collective-permute-start(bf16[384,512]{1,0:T(8,128)(2,1)S(1)} %attend0_odd.1.before_odd), channel_id=1, source_target_pairs={{8,16},{24,32},{40,48},{56,64},{72,80},{88,96},{104,112},{120,128}... | collective-permute-start | bytes 1179656 | tf_op jit(solution)/shard_map/ppermute | solution.py:321
  59.1 5.9 %collective-permute-start.1 = (bf16[384,512]{1,0:T(8,128)(2,1)S(1)}, bf16[384,512]{1,0:T(8,128)(2,1)S(1)}, u32[]{:S(2)}, u32[]{:S(2)}) collective-permute-start(bf16[384,512]{1,0:T(8,128)(2,1)S(1)} %attend0_even.1.before_even), channel_id=1, source_target_pairs={{0,8},{16,24},{32,40},{48,56},{64,72},{80,88},{96,104},{112,120},{... | collective-permute-start | bytes 1179656 | tf_op jit(solution)/shard_map/ppermute | solution.py:321

commit v5 on v4

--- a/solution.py
+++ b/solution.py
@@ -225,7 +225,7 @@
             out[to, rows, :] = value
 
 
-def attention(gathered, lengths, attended):
+def attention(gathered, lengths, attended, after):
     first = lengths[0]
     second = first + lengths[1]
     third = second + lengths[2]
@@ -250,6 +250,7 @@
             attended[at:count, h * HEAD : (h + 1) * HEAD] = (
                 summed[:, :HEAD] / summed[:, HEAD:]
             ).astype(BF16)
+        after(slice(at, count))
 
 
 def carried_panels(coef, mixed):
@@ -258,12 +259,14 @@
     return dot(first, upper) + dot_t(second, cross), dot(first, cross) + dot(second, lower)
 
 
-def boundary_panels(carried, attended, mixed):
+def boundary_tile(carried, attended, mixed, rows):
     columns = PANEL // HEAD
     return [
         (
-            carried[panel]
-            + dot(attended[...], unpack(mixed, M_AT + panel * columns * M_OWN, M_OWN, columns))
+            carried[panel][rows]
+            + dot(
+                attended[rows, :], unpack(mixed, M_AT + panel * columns * M_OWN, M_OWN, columns)
+            )
         ).astype(BF16)
         for panel in range(RANK // PANEL)
     ]
@@ -276,9 +279,12 @@
         copy.start()
         carried = carried_panels(coef[...], gathered)
         copy.wait()
-        attention(gathered, [lengths[0, 0, i] for i in range(3)], attended)
-        for panel, value in enumerate(boundary_panels(carried, attended, gathered)):
-            out[:, panel * PANEL : (panel + 1) * PANEL] = value
+
+        def after(rows):
+            for panel, value in enumerate(boundary_tile(carried, attended, gathered, rows)):
+                out[rows, panel * PANEL : (panel + 1) * PANEL] = value
+
+        attention(gathered, [lengths[0, 0, i] for i in range(3)], attended, after)
 
 
 def second_kernel(
@@ -295,16 +301,18 @@
     copies = []
     carried = carried_panels(coef_a[...] + coef_b[...], mixed)
     lengths_copy.wait()
-    attention(gathered, [lengths[0, 1, i] for i in range(3)], attended)
-    for panel, value in enumerate(boundary_panels(carried, attended, mixed)):
-        columns = pl.ds(panel * PANEL, PANEL)
-        buffer[:, columns] = value
-        copies.append(
-            pltpu.make_async_copy(
-                buffer.at[:, columns], out.at[1, :, columns], sems.at[1 + panel]
-            )
+
+    def after(rows):
+        for panel, value in enumerate(boundary_tile(carried, attended, mixed, rows)):
+            buffer[rows, panel * PANEL : (panel + 1) * PANEL] = value
+        place = pl.ds(rows.start, HEAD)
+        copy = pltpu.make_async_copy(
+            buffer.at[place], out.at[1, place], sems.at[(1, 2, 5)[len(copies)]]
         )
-        copies[-1].start()
+        copy.start()
+        copies.append(copy)
+
+    attention(gathered, [lengths[0, 1, i] for i in range(3)], attended, after)
     for copy in copies:
         copy.wait()
     pl.when(odd)(from_odd.wait)
@@ -373,7 +381,7 @@
         second_kernel, "attend1", shape((2, ROWS, RANK), BF16), [VMEM] * 6 + [ANY],
         attend_flops, 4 * MIB,
         (heads, mixed, *coef1, boundary_odd, boundary_even, doc_lengths),
-        [attended, pltpu.VMEM((ROWS, RANK), BF16), lengths, pltpu.SemaphoreType.DMA((5,))], HBM,
+        [attended, pltpu.VMEM((ROWS, RANK), BF16), lengths, pltpu.SemaphoreType.DMA((6,))], HBM,
     )
     return both[None]
 

time: 101 us -> 102 us (level)
  no operation moved by 1% of the time
where the time goes in v5:
time: 102 us; the launch traced here: 101 us
  blocking collectives  82.2 us (81%)
  Pallas kernels  11.8 us (12%)
  starting transfers between devices  5.85 us (6%)
  waiting for transfers between devices  1.31 us (1%)
    all_to_all x4, blocking collectives, exchange(): return lax.all_to_all(blocks, 'tensor', 0, 0)  82.2 us
    pallas_call x7, Pallas kernels, call(): pl.pallas_call(body, name=name, out_shape=out_shape, in_specs=in_specs, o...  11.8 us
    ppermute x2, starting transfers between devices, hop(): return lax.ppermute(value, 'section', pairs)  5.85 us
  transfers between devices with their start and end apart: 2, of which 2 were waited for; matrix products, arithmetic and copies ran while one was open for 0% of the time, Pallas kernels for 2%

profile of v5, /device:TPU:104, one launch (start us, length us, event | category | flops | bytes accessed | tf_op | source)
XLA Modules:
  0.0 101.3 jit_solution(13508714934090983530)
XLA Ops:
  0.0 4.6 %project0.1 = (bf16[8,720,128]{2,1,0:T(8,128)(2,1)S(1)}, f32[4,48,128]{2,1,0:T(8,128)S(1)}) custom-call(s32[1,2,4]{2,1,0:T(2,128)} %lengths_in.7, bf16[1024,512]{1,0:T(8,128)(2,1)} %basis.1, bf16[512,1024]{1,0:T(8,128)(2,1)} %bitcast.12, bf16[384,512]{1,0:T(8,128)(2,1)} %bitcast.9, bf16[1,2,384,1024]{3,2,1,0:T(8,128)(2,1)} %emb.1, bf16[1,1024]{1,0:T(2,128)(2,1)} %gain.1, ...), custom_call_target="tpu_custom_call" | custom-call | flops 2013265920 | bytes 5242880 | tf_op jit(solution)/shard_map/project0/pallas_call | solution.py:41
  4.6 27.4 %all_to_all.20.parts = bf16[8,720,128]{2,1,0:T(8,128)(2,1)S(1)} all-to-all(bf16[8,720,128]{2,1,0:T(8,128)(2,1)S(1)} %get-tuple-element.7), channel_id=1, replica_groups=mesh['section'=64,'tensor'=8] {'tensor'}, dimensions={0} | all-to-all | bytes 2949120 | tf_op jit(solution)/shard_map/all_to_all | solution.py:323
  32.0 0.3 finish0.1
  32.3 0.0 copy-start.5
  32.3 0.0 copy-start.6
  32.3 23.2 %all_to_all.21.gathered.mixed = bf16[8,704,128]{2,1,0:T(8,128)(2,1)S(1)} all-to-all(bf16[8,704,128]{2,1,0:T(8,128)(2,1)S(1)} %finish0.1), channel_id=1, replica_groups=mesh['section'=64,'tensor'=8] {'tensor'}, dimensions={0} | all-to-all | bytes 2883584 | tf_op jit(solution)/shard_map/all_to_all | solution.py:323
  55.5 0.0 copy-done.5
  55.5 0.0 copy-done.6
  55.5 0.0 copy-start.1
  55.5 0.0 copy-start.2
  55.5 0.0 copy-start
  55.5 0.0 copy-start.3
  55.5 0.0 copy-start.4
  55.6 1.6 %collective-permute-start = (bf16[384,512]{1,0:T(8,128)(2,1)S(1)}, bf16[384,512]{1,0:T(8,128)(2,1)S(1)}, u32[]{:S(2)}, u32[]{:S(2)}) collective-permute-start(bf16[384,512]{1,0:T(8,128)(2,1)S(1)} %attend0_odd.1.before_odd), channel_id=1, source_target_pairs={{8,16},{24,32},{40,48},{56,64},{72,80},{88,96},{104,112},{120,128}... | collective-permute-start | bytes 1179656 | tf_op jit(solution)/shard_map/ppermute | solution.py:329
  57.1 2.3 %attend0_even.1.before_even = bf16[384,512]{1,0:T(8,128)(2,1)S(1)} custom-call(bf16[8,704,128]{2,1,0:T(8,128)(2,1)S(1)} %all_to_all.21.gathered.mixed, bf16[384,512]{1,0:T(8,128)(2,1)S(1)} %bitcast.11, s32[1,2,4]{2,1,0:T(2,128)S(1)} %copy-done.5), custom_call_target="tpu_custom_call" | custom-call | flops 704643072 | bytes 3145728 | tf_op jit(solution)/shard_map/attend0_even/pallas_call | solution.py:41
  59.4 4.3 %collective-permute-start.1 = (bf16[384,512]{1,0:T(8,128)(2,1)S(1)}, bf16[384,512]{1,0:T(8,128)(2,1)S(1)}, u32[]{:S(2)}, u32[]{:S(2)}) collective-permute-start(bf16[384,512]{1,0:T(8,128)(2,1)S(1)} %attend0_even.1.before_even), channel_id=1, source_target_pairs={{0,8},{16,24},{32,40},{48,56},{64,72},{80,88},{96,104},{112,120},{... | collective-permute-start | bytes 1179656 | tf_op jit(solution)/shard_map/ppermute | solution.py:329
  63.7 1.2 %collective-permute-done.coef_a = bf16[384,512]{1,0:T(8,128)(2,1)S(1)} collective-permute-done((bf16[384,512]{1,0:T(8,128)(2,1)S(1)}, bf16[384,512]{1,0:T(8,128)(2,1)S(1)}, u32[]{:S(2)}, u32[]{:S(2)}) %collective-permute-start) | collective-permute-done | bytes 393248 | tf_op jit(solution)/shard_map/ppermute | solution.py:329
  64.9 0.1 collective-permute-done.1.coef_b
  65.1 0.0 copy-done.1
  65.1 0.0 copy-done.2
  65.1 0.0 copy-done
  65.1 0.0 copy-done.3
  65.1 0.0 copy-done.4
  65.1 1.4 %project1.1 = bf16[8,304,128]{2,1,0:T(8,128)(2,1)S(1)} custom-call(bf16[384,512]{1,0:T(8,128)(2,1)S(1)} %collective-permute-done.coef_a, bf16[384,512]{1,0:T(8,128)(2,1)S(1)} %collective-permute-done.1.coef_b, bf16[1,1024]{1,0:T(2,128)(2,1)S(1)} %copy-done.4, bf16[1024,512]{1,0:T(8,128)(2,1)S(1)} %copy-done.1, bf16[1,2,384,1024]{3,2,1,0:T(8,128)(2,1)S(1)} %copy-done, ...), custom_call_target="tpu_custom_call" | custom-call | flops 1006632960 | bytes 5242880 | tf_op jit(solution)/shard_map/project1/pallas_call | solution.py:41
  66.5 16.0 %all_to_all.22.parts = bf16[8,304,128]{2,1,0:T(8,128)(2,1)S(1)} all-to-all(bf16[8,304,128]{2,1,0:T(8,128)(2,1)S(1)} %project1.1), channel_id=1, replica_groups=mesh['section'=64,'tensor'=8] {'tensor'}, dimensions={0} | all-to-all | bytes 1245184 | tf_op jit(solution)/shard_map/all_to_all | solution.py:323
  82.5 0.2 finish1.1
  82.7 15.6 %all_to_all.23.gathered = bf16[8,288,128]{2,1,0:T(8,128)(2,1)S(1)} all-to-all(bf16[8,288,128]{2,1,0:T(8,128)(2,1)S(1)} %finish1.1), channel_id=1, replica_groups=mesh['section'=64,'tensor'=8] {'tensor'}, dimensions={0} | all-to-all | bytes 1179648 | tf_op jit(solution)/shard_map/all_to_all | solution.py:323
  98.3 3.0 %attend1.1 = bf16[2,384,512]{2,1,0:T(8,128)(2,1)} custom-call(bf16[8,288,128]{2,1,0:T(8,128)(2,1)S(1)} %all_to_all.23.gathered, bf16[8,704,128]{2,1,0:T(8,128)(2,1)S(1)} %all_to_all.21.gathered.mixed, bf16[384,512]{1,0:T(8,128)(2,1)S(1)} %collective-permute-done.coef_a, bf16[384,512]{1,0:T(8,128)(2,1)S(1)} %collective-permute-done.1.coef_b, ...), custom_call_target="tpu_custom_call" | custom-call | flops 704643072 | bytes 4194304 | tf_op jit(solution)/shard_map/attend1/pallas_call | solution.py:41
  (1 shorter events, 0.0 us)
Async XLA Ops:
  32.3 23.2 %copy-start.5 = (s32[1,2,4]{2,1,0:T(2,128)S(1)}, s32[1,2,4]{2,1,0:T(2,128)}, u32[]{:S(2)}) copy-start(s32[1,2,4]{2,1,0:T(2,128)} %lengths_in.7) | copy-start | bytes 100
  32.3 23.2 %copy-start.6 = (bf16[1,384,512]{2,1,0:T(8,128)(2,1)S(1)}, bf16[1,384,512]{2,1,0:T(8,128)(2,1)}, u32[]{:S(2)}) copy-start(bf16[1,384,512]{2,1,0:T(8,128)(2,1)} %param.8) | copy-start | bytes 1179652
  55.5 9.6 %copy-start.1 = (bf16[1024,512]{1,0:T(8,128)(2,1)S(1)}, bf16[1024,512]{1,0:T(8,128)(2,1)}, u32[]{:S(2)}) copy-start(bf16[1024,512]{1,0:T(8,128)(2,1)} %basis.1) | copy-start | bytes 3145732
  55.5 9.6 %copy-start.2 = (bf16[1,1024,512]{2,1,0:T(8,128)(2,1)S(1)}, bf16[1,1024,512]{2,1,0:T(8,128)(2,1)}, u32[]{:S(2)}) copy-start(bf16[1,1024,512]{2,1,0:T(8,128)(2,1)} %param.11) | copy-start | bytes 3145732
  55.5 9.6 %copy-start = (bf16[1,2,384,1024]{3,2,1,0:T(8,128)(2,1)S(1)}, bf16[1,2,384,1024]{3,2,1,0:T(8,128)(2,1)}, u32[]{:S(2)}) copy-start(bf16[1,2,384,1024]{3,2,1,0:T(8,128)(2,1)} %emb.1) | copy-start | bytes 4718596
  55.5 9.5 %copy-start.3 = (bf16[1,1024,256]{2,1,0:T(8,128)(2,1)S(1)}, bf16[1,1024,256]{2,1,0:T(8,128)(2,1)}, u32[]{:S(2)}) copy-start(bf16[1,1024,256]{2,1,0:T(8,128)(2,1)} %param.12) | copy-start | bytes 1572868
  55.5 9.5 %copy-start.4 = (bf16[1,1024]{1,0:T(2,128)(2,1)S(1)}, bf16[1,1024]{1,0:T(2,128)(2,1)}, u32[]{:S(2)}) copy-start(bf16[1,1024]{1,0:T(2,128)(2,1)} %gain.1) | copy-start | bytes 6148
  55.6 9.4 %collective-permute-start = (bf16[384,512]{1,0:T(8,128)(2,1)S(1)}, bf16[384,512]{1,0:T(8,128)(2,1)S(1)}, u32[]{:S(2)}, u32[]{:S(2)}) collective-permute-start(bf16[384,512]{1,0:T(8,128)(2,1)S(1)} %attend0_odd.1.before_odd), channel_id=1, source_target_pairs={{8,16},{24,32},{40,48},{56,64},{72,80},{88,96},{104,112},{120,128}... | collective-permute-start | bytes 1179656 | tf_op jit(solution)/shard_map/ppermute | solution.py:329
  59.4 5.6 %collective-permute-start.1 = (bf16[384,512]{1,0:T(8,128)(2,1)S(1)}, bf16[384,512]{1,0:T(8,128)(2,1)S(1)}, u32[]{:S(2)}, u32[]{:S(2)}) collective-permute-start(bf16[384,512]{1,0:T(8,128)(2,1)S(1)} %attend0_even.1.before_even), channel_id=1, source_target_pairs={{0,8},{16,24},{32,40},{48,56},{64,72},{80,88},{96,104},{112,120},{... | collective-permute-start | bytes 1179656 | tf_op jit(solution)/shard_map/ppermute | solution.py:329
